TPU v7x, 32 devices: a whole 2x2x4 slice. The times are simulated.
32 devices in a mesh: rows: 2 (over core), blk: 4 (over z), tp: 4 (over y, x).
Axes of the slice: x: 2, y: 2, z: 4, core: 2. Of those that a mesh axis runs over, the one named last changes fastest.
Arguments:
- tokens: bfloat16 [3072, 768], P(('rows', 'blk'), 'tp'), may hold values from -18 to 18
- cotangent: bfloat16 [3072, 768], P(('rows', 'blk'), 'tp'), may hold values from -54 to 54
- segment_ids: int32 [2, 1536], P('rows'), may hold values from 0 to 1535, as said below
- matrices: float32 [768, 2880], P('tp')
- vectors: float32 [12, 768], P(None, 'tp'), may hold values from -2 to 2
- moment_mat: float32 [768, 2880], P('tp'), may hold values from -64 to 64
- square_mat: float32 [768, 2880], P('tp'), may hold values from 1 to 100
- moment_vec: float32 [12, 768], P(None, 'tp'), may hold values from -64 to 64
- square_vec: float32 [12, 768], P(None, 'tp'), may hold values from 1 to 100
Outputs:
- output: bfloat16 [3072, 768], P(('rows', 'blk'), 'tp')
- input_grad: float32 [3072, 768], P(('rows', 'blk'), 'tp')
- matrix_grad: float32 [768, 2880], P('tp')
- vector_grad: float32 [12, 768], P(None, 'tp')
- new_moment_mat: float32 [768, 2880], P('tp')
- new_square_mat: float32 [768, 2880], P('tp')
- new_moment_vec: float32 [12, 768], P(None, 'tp')
- new_square_vec: float32 [12, 768], P(None, 'tp')
- new_matrices: float32 [768, 2880], P('tp')
- new_vectors: float32 [12, 768], P(None, 'tp')
Inputs may be any that keep to these rules, and one draw needn't show every extreme that they name: `segment_ids`: along each row of 1536 tokens a token's value is the position within the row of its document's first token, so values never fall along a row. One document of each row begins within the row's first 384 tokens, after its first token, and ends within its last 384 tokens, before its last; every other document has at most 512 tokens.
All inputs are finite; a program needn't handle non-finite values.
Results may differ from a plain program's by a relative error of at most 0.017.
Values may be sent and summed in bfloat16 or wider, within the bound.
A program may use at most 128 MiB of HBM per device.

v0:
```python
from functools import partial

import jax
import jax.numpy as jnp
from jax import lax
from jax.sharding import PartitionSpec as P

HD = 64
HG = 768


eps_norm = 1e-12
beta_one = 0.9
beta_two = 0.999
adam_eps = 1e-06
step_count = 100.0
decay_rate = 0.01
learn_rate = 0.04
matrix_rate = 1.0


def block_rows(tok_count, total_rows):
    shards = total_rows // tok_count
    return tok_count * next(
        (
            part_count
            for part_count in range(1, shards + 1)
            if shards % part_count == 0 and (tok_count * part_count >= 512 or part_count == shards)
        )
    )


def layer_stats(hidden, model_width):
    center_mean = lax.psum(jnp.sum(hidden, 1), "tp") / model_width
    centered = hidden - center_mean[:, None]
    variance = lax.psum(jnp.sum(centered * centered, 1), "tp") / model_width
    inverse = lax.rsqrt(variance + eps_norm)
    normed = (hidden - center_mean[:, None]) * inverse[:, None]
    return (normed, inverse)


def norm_back(gradient, normed, inverse, gain, model_width):
    scaled = gradient * gain
    first_sum, second_sum = lax.psum((jnp.sum(scaled, 1), jnp.sum(scaled * normed, 1)), "tp")
    return inverse[:, None] * (
        scaled - first_sum[:, None] / model_width - normed * (second_sum / model_width)[:, None]
    )


def lamb_moments(gradient, first_moment, second_moment):
    first_new = beta_one * first_moment + (1.0 - beta_one) * gradient
    second_new = beta_two * second_moment + (1.0 - beta_two) * gradient * gradient
    update = (
        first_new
        / (1.0 - beta_one**step_count)
        / (jnp.sqrt(second_new / (1.0 - beta_two**step_count)) + adam_eps)
    )
    return (first_new, second_new, update)


def local(
    tokens,
    cotangent,
    segment_ids,
    matrices,
    vectors,
    moment_mat,
    square_mat,
    moment_vec,
    square_vec,
):
    f32 = jnp.float32
    bf16 = jnp.bfloat16
    tok_count = tokens.shape[0]
    group_width = tokens.shape[1]
    model_width = group_width * lax.axis_size("tp")
    total_rows = tok_count * lax.axis_size("blk")
    head_count = group_width // HD
    scaling = HD ** (-0.5)
    weights = matrices.astype(bf16)
    w_qkv = weights[:, : 3 * group_width]
    w_out = weights[:, 3 * group_width : 3 * group_width + model_width]
    w_hidden = weights[:, 3 * group_width + model_width : 3 * group_width + model_width + HG]
    w_back = weights[:, 3 * group_width + model_width + HG :]
    ids_row = segment_ids[0]
    ids_local = lax.dynamic_slice_in_dim(ids_row, lax.axis_index("blk") * tok_count, tok_count)
    rows_block = block_rows(tok_count, total_rows)
    block_count = total_rows // rows_block
    ids_blocks = ids_row.reshape(block_count, rows_block)
    bias_qkv = jnp.concatenate([vectors[0], jnp.zeros_like(vectors[0]), vectors[1]])
    projected = (jnp.dot(tokens, w_qkv, preferred_element_type=f32) + bias_qkv).astype(bf16)
    queries = projected[:, :group_width]
    keys_local = projected[:, group_width : 2 * group_width]
    values_local = projected[:, 2 * group_width :]
    key_all, value_all = (
        lax.all_gather(keys_local, "blk", axis=0, tiled=True),
        lax.all_gather(values_local, "blk", axis=0, tiled=True),
    )
    query_heads = queries.reshape(tok_count, head_count, HD)

    def by_block(field):
        return field.reshape(block_count, rows_block, head_count, HD)

    def scores_of(kblock, idblock):
        raw_scores = (
            jnp.einsum("thd,khd->htk", query_heads, kblock, preferred_element_type=f32) * scaling
        )
        same_doc = (ids_local[:, None] == idblock[None, :])[None]
        return (raw_scores, same_doc)

    def top_step(running, pieces):
        running_top, total_mass = running
        kblock, idblock = pieces
        raw_scores, same_doc = scores_of(kblock, idblock)
        masked = jnp.where(same_doc, raw_scores, -1e30)
        new_top = jnp.maximum(running_top, jnp.max(masked, axis=2))
        terms = jnp.where(same_doc, jnp.exp(masked - new_top[:, :, None]), 0.0)
        total_mass = total_mass * jnp.exp(running_top - new_top) + jnp.sum(terms, axis=2)
        return ((new_top, total_mass), None)

    start_top = jnp.full((head_count, tok_count), -1e30, f32)
    start_mass = jnp.zeros((head_count, tok_count), f32)
    (running_top, total_mass), _ = lax.scan(
        top_step, (start_top, start_mass), (by_block(key_all), ids_blocks)
    )
    log_total = running_top + jnp.log(total_mass)

    def probs_of(kblock, idblock):
        raw_scores, same_doc = scores_of(kblock, idblock)
        return jnp.where(same_doc, jnp.exp(raw_scores - log_total[:, :, None]), 0.0)

    def context_step(context_sum, pieces):
        kblock, vblock, idblock = pieces
        attn_probs = probs_of(kblock, idblock).astype(bf16)
        return (
            context_sum
            + jnp.einsum("htk,khd->thd", attn_probs, vblock, preferred_element_type=f32),
            None,
        )

    context_sum, _ = lax.scan(
        context_step,
        jnp.zeros((tok_count, head_count, HD), f32),
        (by_block(key_all), by_block(value_all), ids_blocks),
    )
    context = context_sum.reshape(tok_count, group_width).astype(bf16)
    partial_out = jnp.dot(context, w_out, preferred_element_type=f32)
    attended = (
        lax.psum_scatter(
            partial_out.astype(jnp.bfloat16), "tp", scatter_dimension=1, tiled=True
        ).astype(jnp.float32)
        + vectors[2]
    )
    normed_one, inverse_one = layer_stats(tokens.astype(f32) + attended, model_width)
    middle = normed_one * vectors[3] + vectors[4]
    middle_low = middle.astype(bf16)
    bias_rows = HG // group_width
    pre_act = jnp.dot(middle_low, w_hidden, preferred_element_type=f32) + vectors[
        5 : 5 + bias_rows
    ].reshape(-1)
    activated = jax.nn.gelu(pre_act, approximate=False).astype(bf16)
    ffn_out = (
        jnp.einsum("nj,cj->nc", activated, w_back, preferred_element_type=f32)
        + vectors[5 + bias_rows]
    )
    normed_two, inverse_two = layer_stats(middle + ffn_out, model_width)
    output = (normed_two * vectors[6 + bias_rows] + vectors[7 + bias_rows]).astype(bf16)
    grad_out = cotangent.astype(f32)
    grad_gain_two = jnp.sum(grad_out * normed_two, 0)
    grad_shift_two = jnp.sum(grad_out, 0)
    grad_two = norm_back(grad_out, normed_two, inverse_two, vectors[6 + bias_rows], model_width)
    grad_ffn = grad_two.astype(bf16)
    grad_wback = jnp.einsum("nc,nj->cj", grad_ffn, activated, preferred_element_type=f32)
    grad_bias_back = jnp.sum(grad_ffn, 0, dtype=f32)
    grad_act = jnp.dot(grad_ffn, w_back, preferred_element_type=f32)
    _, gelu_pull = jax.vjp(partial(jax.nn.gelu, approximate=False), pre_act)
    grad_pre = gelu_pull(grad_act)[0].astype(bf16)
    grad_whidden = jnp.einsum("ni,nj->ij", middle_low, grad_pre, preferred_element_type=f32)
    grad_bias_hidden = jnp.sum(grad_pre, 0, dtype=f32).reshape(bias_rows, group_width)
    grad_middle = grad_two + jnp.einsum("nj,ij->ni", grad_pre, w_hidden, preferred_element_type=f32)
    grad_gain_one = jnp.sum(grad_middle * normed_one, 0)
    grad_shift_one = jnp.sum(grad_middle, 0)
    grad_one = norm_back(grad_middle, normed_one, inverse_one, vectors[3], model_width)
    grad_attended = grad_one.astype(bf16)
    grad_bias_out = jnp.sum(grad_attended, 0, dtype=f32)
    grad_attended_all = lax.all_gather(grad_attended, "tp", axis=1, tiled=True)
    grad_wout = jnp.einsum("nc,ne->ce", context, grad_attended_all, preferred_element_type=f32)
    grad_context = jnp.einsum(
        "ne,ce->nc", grad_attended_all, w_out, preferred_element_type=f32
    ).astype(bf16)
    key_back, value_back = (
        lax.all_gather(keys_local, "blk", axis=0, tiled=True),
        lax.all_gather(values_local, "blk", axis=0, tiled=True),
    )
    grad_heads = grad_context.reshape(tok_count, head_count, HD)

    def delta_step(row_delta, pieces):
        kblock, vblock, idblock = pieces
        attn_probs = probs_of(kblock, idblock)
        grad_probs = jnp.einsum("thd,khd->htk", grad_heads, vblock, preferred_element_type=f32)
        return (row_delta + jnp.sum(attn_probs * grad_probs, 2), None)

    row_delta, _ = lax.scan(
        delta_step,
        jnp.zeros((head_count, tok_count), f32),
        (by_block(key_back), by_block(value_back), ids_blocks),
    )

    def score_grads(kblock, vblock, idblock):
        attn_probs = probs_of(kblock, idblock)
        grad_probs = jnp.einsum("thd,khd->htk", grad_heads, vblock, preferred_element_type=f32)
        grad_scores = (attn_probs * (grad_probs - row_delta[:, :, None])).astype(bf16)
        return (attn_probs, grad_scores)

    start_sum = jnp.zeros((tok_count, head_count, HD), f32)

    def grad_step(grad_sum, pieces):
        kblock, vblock, idblock = pieces
        attn_probs, grad_scores = score_grads(kblock, vblock, idblock)
        grad_sum = grad_sum + jnp.einsum(
            "htk,khd->thd", grad_scores, kblock, preferred_element_type=f32
        )
        key_term = jnp.einsum(
            "htk,thd->khd", grad_scores, query_heads, preferred_element_type=f32
        ).reshape(rows_block, group_width)
        value_term = jnp.einsum(
            "htk,thd->khd", attn_probs.astype(bf16), grad_heads, preferred_element_type=f32
        ).reshape(rows_block, group_width)
        return (grad_sum, (key_term, value_term))

    grad_sum, (key_terms, value_terms) = lax.scan(
        grad_step, start_sum, (by_block(key_back), by_block(value_back), ids_blocks)
    )
    grad_key, grad_value = (
        lax.psum_scatter(
            (key_terms.reshape(total_rows, group_width) * scaling).astype(jnp.bfloat16),
            "blk",
            scatter_dimension=0,
            tiled=True,
        ).astype(jnp.float32),
        lax.psum_scatter(
            value_terms.reshape(total_rows, group_width).astype(jnp.bfloat16),
            "blk",
            scatter_dimension=0,
            tiled=True,
        ).astype(jnp.float32),
    )
    grad_query = (grad_sum * scaling).reshape(tok_count, group_width).astype(bf16)
    grad_qkv = jnp.concatenate([grad_query, grad_key.astype(bf16), grad_value.astype(bf16)], 1)
    grad_wqkv = jnp.einsum("ni,nk->ik", tokens, grad_qkv, preferred_element_type=f32)
    input_grad = grad_one + jnp.einsum("nk,ik->ni", grad_qkv, w_qkv, preferred_element_type=f32)
    qkv_sums = jnp.sum(grad_qkv, 0, dtype=f32)
    local_mat = jnp.concatenate([grad_wqkv, grad_wout, grad_whidden, grad_wback], 1)
    local_vec = jnp.concatenate(
        [
            qkv_sums[None, :group_width],
            qkv_sums[None, 2 * group_width :],
            grad_bias_out[None],
            grad_gain_one[None],
            grad_shift_one[None],
            grad_bias_hidden,
            grad_bias_back[None],
            grad_gain_two[None],
            grad_shift_two[None],
        ],
        0,
    )
    matrix_grad, vector_grad = lax.psum((local_mat, local_vec), ("rows", "blk"))
    new_moment_mat, new_square_mat, update_mat = lamb_moments(matrix_grad, moment_mat, square_mat)
    update_mat = update_mat + decay_rate * matrices
    bounds = [
        0,
        group_width,
        2 * group_width,
        3 * group_width,
        3 * group_width + model_width,
        3 * group_width + model_width + HG,
        matrices.shape[1],
    ]
    col_lower = jnp.array(bounds[:-1], jnp.int32)
    col_upper = jnp.array(bounds[1:], jnp.int32)
    columns = lax.iota(jnp.int32, matrices.shape[1])
    member = (
        (columns[:, None] >= col_lower[None, :]) & (columns[:, None] < col_upper[None, :])
    ).astype(f32)
    weight_cols = jnp.sum(matrices * matrices, 0)
    update_cols = jnp.sum(update_mat * update_mat, 0)
    weight_sq, update_sq = lax.psum(
        (
            jnp.dot(weight_cols, member, precision=lax.Precision.HIGHEST),
            jnp.dot(update_cols, member, precision=lax.Precision.HIGHEST),
        ),
        "tp",
    )
    trust_ratio = jnp.sqrt(weight_sq / (update_sq + 1e-12))
    ratio_cols = jnp.dot(member, trust_ratio, precision=lax.Precision.HIGHEST)
    new_matrices = matrices - matrix_rate * ratio_cols[None, :] * update_mat
    new_moment_vec, new_square_vec, update_vec = lamb_moments(vector_grad, moment_vec, square_vec)
    new_vectors = vectors - learn_rate * update_vec
    return (
        output,
        input_grad,
        matrix_grad,
        vector_grad,
        new_moment_mat,
        new_square_mat,
        new_moment_vec,
        new_square_vec,
        new_matrices,
        new_vectors,
    )


def solution(mesh):
    return jax.shard_map(
        local,
        mesh=mesh,
        in_specs=(
            P(("rows", "blk"), "tp"),
            P(("rows", "blk"), "tp"),
            P("rows", None),
            P("tp", None),
            P(None, "tp"),
            P("tp", None),
            P("tp", None),
            P(None, "tp"),
            P(None, "tp"),
        ),
        out_specs=(
            P(("rows", "blk"), "tp"),
            P(("rows", "blk"), "tp"),
            P("tp", None),
            P(None, "tp"),
            P("tp", None),
            P("tp", None),
            P(None, "tp"),
            P(None, "tp"),
            P("tp", None),
            P(None, "tp"),
        ),
        check_vma=False,
    )
```

profile of v0, /device:TPU:0, one launch (start us, length us, event | category | flops | bytes accessed | tf_op | source)
XLA Modules:
  0.0 334.0 jit_solution(16901008717613306654)
XLA Ops:
  11.9 18.3 %all_gather.12 = bf16[1536,192]{0,1:T(8,128)(2,1)S(1)} all-gather(bf16[384,192]{0,1:T(8,128)(2,1)S(1)} %get-tuple-element.574), channel_id=1, replica_groups=mesh['rows'=2,'blk'=4,'tp'=4] {'blk'}, dimensions={0}, use_global_device_ids=true | all-gather | bytes 737280 | tf_op jit(solution)/shard_map/all_gather | solution.py:96
  32.3 4.1 %while.50 = (s32[]{:T(128)}, f32[3,384]{1,0:T(4,128)S(1)}, f32[3,384]{1,0:T(4,128)S(1)}, s32[384]{0:T(512)S(1)}, s32[2,768]{1,0:T(2,128)S(1)}, /*index=5*/bf16[2...) while((s32[]{:T(128)}, f32[3,384]{1,0:T(4,128)S(1)}, ...), condition=%wide.region_3.4_spmd.clone, body=%wide.region_0.3_spmd.clone.sunk | while | flops 120624768 | bytes 8475768 | solution.py:123
  36.5 16.5 %all_gather.11 = bf16[1536,192]{0,1:T(8,128)(2,1)S(1)} all-gather(bf16[384,192]{0,1:T(8,128)(2,1)S(1)} %get-tuple-element.575), channel_id=1, replica_groups=mesh['rows'=2,'blk'=4,'tp'=4] {'blk'}, dimensions={0}, use_global_device_ids=true | all-gather | bytes 737280 | tf_op jit(solution)/shard_map/all_gather | solution.py:97
  55.1 2.9 while.51
  61.7 26.3 %reduce-scatter.8.cloned.1.call-done = bf16[384,192]{0,1:T(8,128)(2,1)} async-done(((bf16[384,768]{0,1:T(8,128)(2,1)}), bf16[384,192]{0,1:T(8,128)(2,1)}) %reduce-scatter.8.cloned.1.call-update) | async-done | bytes 147472 | tf_op jit(solution)/shard_map/reduce_scatter | solution.py:149
  89.0 8.9 %psum.84 = f32[384]{0:T(512)S(1)} all-reduce(f32[384]{0:T(512)S(1)} %fusion.69), channel_id=1, replica_groups=mesh['rows'=2,'blk'=4,'tp'=4] {'tp'}, use_global_device_ids=true, to_apply=%region_8.9 | all-reduce | flops 384 | bytes 3072 | tf_op jit(solution)/shard_map/psum | solution.py:34
  99.0 8.8 %psum.85 = f32[384]{0:T(512)S(1)} all-reduce(f32[384]{0:T(512)S(1)} %multiply_reduce_fusion.5), channel_id=1, replica_groups=mesh['rows'=2,'blk'=4,'tp'=4] {'tp'}, use_global_device_ids=true, to_apply=%region_10.11 | all-reduce | flops 384 | bytes 3072 | tf_op jit(solution)/shard_map/psum | solution.py:36
  107.8 5.3 %multiply_convert_fusion.1 = (bf16[384,768]{1,0:T(8,128)(2,1)S(1)}, f32[384,768]{1,0:T(8,128)}, f32[384,768]{1,0:T(8,128)}) fusion(f32[768]{0:T(1024)S(1)} %add.178, bf16[192,2880]{1,0:T(8,128)(2,1)S(1)} %convert_element_type.90, f32[192]{0:T(256)S(1)} %bitcast.228, f32[192]{0:T(256)S(1)} %bitcast.219, f32[384]{0:T(512)S(1)} %add_rsqrt_fusion.1, ...), kind=kOutput, calls=%fused_computation.80 | convolution fusion | flops 133373952 | bytes 3550208 | tf_op jit(solution)/shard_map/dot_general | solution.py:158
  114.4 8.9 %psum.86 = f32[384]{0:T(512)S(1)} all-reduce(f32[384]{0:T(512)S(1)} %get-tuple-element.588), channel_id=1, replica_groups=mesh['rows'=2,'blk'=4,'tp'=4] {'tp'}, use_global_device_ids=true, to_apply=%region_12.13 | all-reduce | flops 384 | bytes 3072 | tf_op jit(solution)/shard_map/psum | solution.py:34
  123.3 8.0 %psum.87 = f32[384]{0:T(512)S(1)} all-reduce(f32[384]{0:T(512)S(1)} %multiply_reduce_fusion.4), channel_id=1, replica_groups=mesh['rows'=2,'blk'=4,'tp'=4] {'tp'}, use_global_device_ids=true, to_apply=%region_14.15 | all-reduce | flops 384 | bytes 3072 | tf_op jit(solution)/shard_map/psum | solution.py:36
  131.6 8.9 %all-reduce.2 = (f32[384]{0:T(512)S(1)}, f32[384]{0:T(512)S(1)}) all-reduce(f32[384]{0:T(512)S(1)} %get-tuple-element.477, f32[384]{0:T(512)S(1)} %get-tuple-element.480), channel_id=1, replica_groups=mesh['rows'=2,'blk'=4,'tp'=4] {'tp'}, use_global_device_ids=true, to_apply=%region_18.19 | all-reduce | flops 768 | bytes 6144 | tf_op jit(solution)/shard_map/psum | solution.py:44
  141.4 2.5 convert_reduce_fusion
  144.7 8.8 %all-reduce.1 = (f32[384]{0:T(512)S(1)}, f32[384]{0:T(512)S(1)}) all-reduce(f32[384]{0:T(512)S(1)} %get-tuple-element.475, f32[384]{0:T(512)S(1)} %get-tuple-element.478), channel_id=1, replica_groups=mesh['rows'=2,'blk'=4,'tp'=4] {'tp'}, use_global_device_ids=true, to_apply=%region_22.23 | all-reduce | flops 768 | bytes 6144 | tf_op jit(solution)/shard_map/psum | solution.py:44
  153.9 9.6 %all_gather.13 = bf16[384,768]{0,1:T(8,128)(2,1)S(1)} all-gather(bf16[384,192]{0,1:T(8,128)(2,1)S(1)} %get-tuple-element.568), channel_id=1, replica_groups=mesh['rows'=2,'blk'=4,'tp'=4] {'tp'}, dimensions={1}, use_global_device_ids=true | all-gather | bytes 737280 | tf_op jit(solution)/shard_map/all_gather | solution.py:186
  164.5 5.5 %while.52 = (s32[]{:T(128)}, f32[3,384]{1,0:T(4,128)S(1)}, s32[384]{0:T(512)S(1)}, s32[2,768]{1,0:T(2,128)S(1)}, bf16[2,768,3,64]{1,3,2,0:T(8,128)(2,1)S(1)}, /*...) while((s32[]{:T(128)}, f32[3,384]{1,0:T(4,128)S(1)}, ...), condition=%wide.region_25.26_spmd.clone, body=%wide.region_23.25_spmd.clone.sunk | while | flops 231212160 | bytes 11537091 | solution.py:203
  170.1 12.0 %while.53 = (s32[]{:T(128)}, f32[384,3,64]{0,2,1:T(8,128)S(1)}, f32[2,768,192]{1,2,0:T(8,128)S(1)}, bf16[2,768,192]{1,2,0:T(8,128)(2,1)}, bf16[2,768,3,64]{1,3,2...) while((s32[]{:T(128)}, f32[384,3,64]{0,2,1:T(8,128)S(1)}, ...), condition=%wide.region_27.28_spmd.clone, body=%wide.region_26.27_spmd.clone.sunk | while | flops 575520768 | bytes 29224224 | solution.py:231
  187.1 20.6 %reduce-scatter.12.cloned.1.call-done = bf16[384,192]{1,0:T(8,128)(2,1)} async-done(((bf16[1536,192]{1,0:T(8,128)(2,1)}), bf16[384,192]{1,0:T(8,128)(2,1)}) %reduce-scatter.12.cloned.1.call-update) | async-done | bytes 147472
  208.9 24.5 %reduce-scatter.10.cloned.1.call-done = bf16[384,192]{1,0:T(8,128)(2,1)} async-done(((bf16[1536,192]{1,0:T(8,128)(2,1)}), bf16[384,192]{1,0:T(8,128)(2,1)}) %reduce-scatter.10.cloned.1.call-update) | async-done | bytes 147472
  234.8 2.3 concatenate.14
  237.6 28.0 %psum.93 = f32[12,192]{1,0:T(8,128)S(1)} all-reduce(f32[12,192]{1,0:T(8,128)S(1)} %concatenate.15), channel_id=1, replica_groups=mesh['rows'=2,'blk'=4,'tp'=4] {'rows','blk'}, use_global_device_ids=true, to_apply=%region_39.40 | all-reduce | flops 2304 | bytes 18432 | tf_op jit(solution)/shard_map/psum | solution.py:268
  267.7 35.0 %all-reduce.5.cloned.1.call-done = f32[192,2880]{1,0:T(8,128)} async-done(((f32[192,2880]{1,0:T(8,128)}), f32[192,2880]{1,0:T(8,128)}) %all-reduce.5.cloned.1.call-update) | async-done | bytes 2211856 | tf_op jit(solution)/shard_map/psum | solution.py:268
  302.7 7.0 %multiply_reduce_fusion = (f32[2880]{0:T(1024)S(1)}, f32[2880]{0:T(1024)S(1)}, f32[192,2880]{1,0:T(8,128)}, f32[192,2880]{1,0:T(8,128)}) fusion(f32[192,2880]{1,0:T(8,128)S(1)} %copy-done, f32[192,2880]{1,0:T(8,128)} %all-reduce.5.cloned.1.call-done, f32[192,2880]{1,0:T(8,128)} %param.25, f32[192,2880]{1,0:T(8,128)} %param.24), kind=kLoop, calls=%fused_computation.66 | loop fusion | flops 9394560 | bytes 13294080 | tf_op jit(solution)/shard_map/reduce_sum | solution.py:287
  310.9 9.9 %all-reduce = (f32[6]{0:T(128)S(1)}, f32[6]{0:T(128)S(1)}) all-reduce(f32[6]{0:T(128)S(1)} %convolution_bitcast_fusion.3, f32[6]{0:T(128)S(1)} %convolution_bitcast_fusion.2), channel_id=1, replica_groups=mesh['rows'=2,'blk'=4,'tp'=4] {'tp'}, use_global_device_ids=true, to_apply=%region_41.42 | all-reduce | flops 12 | bytes 96 | tf_op jit(solution)/shard_map/psum | solution.py:288
  321.1 5.0 %multiply_subtract_fusion = f32[192,2880]{1,0:T(8,128)} fusion(f32[192,2880]{1,0:T(8,128)S(1)} %copy-done, f32[2880]{0:T(1024)S(1)} %convolution_reduce_fusion, f32[192,2880]{1,0:T(8,128)} %get-tuple-element.956, f32[192,2880]{1,0:T(8,128)} %get-tuple-element.955), kind=kLoop, calls=%fused_computation.65 | loop fusion | flops 4423680 | bytes 8858880 | tf_op jit(solution)/shard_map/sub | solution.py:297
  (193 shorter events, 56.0 us)
Async XLA Ops:
  7.2 80.8 %reduce-scatter.8.cloned.1.call-start = ((), (), s32[]{:S(2)}) async-start(), calls=%async_computation.3 | async-start | bytes 737280 | tf_op jit(solution)/shard_map/reduce_scatter | solution.py:149
  9.6 1.9 copy-start.3
  11.4 152.1 %copy-start.2 = (bf16[192,2880]{1,0:T(8,128)(2,1)}, bf16[192,2880]{1,0:T(8,128)(2,1)S(1)}, u32[]{:S(2)}) copy-start(bf16[192,2880]{1,0:T(8,128)(2,1)S(1)} %convert_element_type.90) | copy-start | bytes 3317764
  53.0 2.1 copy-start.21
  58.7 30.2 %copy-start.9 = (bf16[2,768,3,64]{1,3,2,0:T(8,128)(2,1)}, bf16[2,768,3,64]{1,3,2,0:T(8,128)(2,1)S(1)}, u32[]{:S(2)}) copy-start(bf16[2,768,3,64]{1,3,2,0:T(8,128)(2,1)S(1)} %get-tuple-element.987) | copy-start | bytes 1769476
  58.7 2.8 copy-start.26
  61.5 146.3 %reduce-scatter.12.cloned.1.call-start = ((), (), s32[]{:S(2)}) async-start(), calls=%async_computation.6 | async-start | bytes 983040
  107.8 6.1 %copy-start.4 = (bf16[384,192]{0,1:T(8,128)(2,1)S(1)}, bf16[384,192]{0,1:T(8,128)(2,1)}, u32[]{:S(2)}) copy-start(bf16[384,192]{0,1:T(8,128)(2,1)} %reduce-scatter.8.cloned.1.call-done) | copy-start | bytes 442372
  113.1 18.3 %copy-start.12 = (bf16[384,192]{0,1:T(8,128)(2,1)S(1)}, bf16[384,192]{0,1:T(8,128)(2,1)}, u32[]{:S(2)}) copy-start(bf16[384,192]{0,1:T(8,128)(2,1)} %param.20) | copy-start | bytes 442372
  141.4 2.5 copy-start.17
  144.7 9.1 %copy-start.19 = (f32[384,192]{0,1:T(8,128)}, f32[384,192]{0,1:T(8,128)S(1)}, u32[]{:S(2)}) copy-start(f32[384,192]{0,1:T(8,128)S(1)} %get-tuple-element.590) | copy-start | bytes 884740
  164.5 5.5 %copy-start.6 = (f32[2,768,192]{1,2,0:T(8,128)S(1)}, f32[2,768,192]{1,2,0:T(8,128)}, u32[]{:S(2)}) copy-start(f32[2,768,192]{1,2,0:T(8,128)} %custom-call.5) | copy-start | bytes 3538948
  184.3 49.1 %reduce-scatter.10.cloned.1.call-start = ((), (), s32[]{:S(2)}) async-start(), calls=%async_computation.5 | async-start | bytes 983040
  184.4 1.3 copy-start.14
  185.6 117.1 %all-reduce.5.cloned.1.call-start = ((), (), s32[]{:S(2)}) async-start(), calls=%async_computation.4 | async-start | bytes 4521984 | tf_op jit(solution)/shard_map/psum | solution.py:268
  237.1 28.4 %copy-start.5 = (bf16[384,192]{0,1:T(8,128)(2,1)S(1)}, bf16[384,192]{0,1:T(8,128)(2,1)}, u32[]{:S(2)}) copy-start(bf16[384,192]{0,1:T(8,128)(2,1)} %reduce-scatter.8.cloned.1.call-done) | copy-start | bytes 442372
  237.1 28.4 %copy-start.20 = (f32[384,192]{0,1:T(8,128)S(1)}, f32[384,192]{0,1:T(8,128)}, u32[]{:S(2)}) copy-start(f32[384,192]{0,1:T(8,128)} %copy-done.19) | copy-start | bytes 884740
  265.6 44.7 %copy-start.25 = (f32[12,192]{1,0:T(8,128)}, f32[12,192]{1,0:T(8,128)S(1)}, u32[]{:S(2)}) copy-start(f32[12,192]{1,0:T(8,128)S(1)} %psum.93) | copy-start | bytes 27652
  265.6 37.1 %copy-start = (f32[192,2880]{1,0:T(8,128)S(1)}, f32[192,2880]{1,0:T(8,128)}, u32[]{:S(2)}) copy-start(f32[192,2880]{1,0:T(8,128)} %param.22) | copy-start | bytes 6635524
  267.7 42.0 %copy-start.29 = (s32[6]{0:T(128)S(1)}, s32[6]{0:T(128)}, u32[]{:S(2)}) copy-start(s32[6]{0:T(128)} %constant.188.clone) | copy-start | bytes 76
  267.7 42.0 %copy-start.30 = (s32[6]{0:T(128)S(1)}, s32[6]{0:T(128)}, u32[]{:S(2)}) copy-start(s32[6]{0:T(128)} %constant.187.clone) | copy-start | bytes 76
  267.7 42.5 %copy-start.27 = (f32[12,192]{1,0:T(8,128)S(1)}, f32[12,192]{1,0:T(8,128)}, u32[]{:S(2)}) copy-start(f32[12,192]{1,0:T(8,128)} %param.27) | copy-start | bytes 27652
  267.7 42.6 %copy-start.28 = (f32[12,192]{1,0:T(8,128)S(1)}, f32[12,192]{1,0:T(8,128)}, u32[]{:S(2)}) copy-start(f32[12,192]{1,0:T(8,128)} %param.26) | copy-start | bytes 27652
  321.1 5.0 %copy-start.1 = (f32[192,2880]{1,0:T(8,128)S(1)}, f32[192,2880]{1,0:T(8,128)}, u32[]{:S(2)}) copy-start(f32[192,2880]{1,0:T(8,128)} %all-reduce.5.cloned.1.call-done) | copy-start | bytes 6635524
  (17 other events, 16.9 us)
Sparse Core Ops, SparseCore 0:
  61.6 26.2 reduce-scatter.7
  184.4 23.3 reduce-scatter.11
  210.8 22.5 reduce-scatter.9
  237.3 65.3 all-reduce.4
where the time goes:
time: 335 us; the launch traced here: 334 us
  blocking collectives  135 us (40%)
  waiting for transfers between devices  106 us (32%)
  matrix products  32.2 us (10%)
  other arithmetic  24 us (7%)
  local copies, waits for them, and re-layouts  21.7 us (6%)
  between operations  14.3 us (4%)
    unnamed x6, waiting for transfers between devices  45.2 us
    psum x1, waiting for transfers between devices, local(): matrix_grad, vector_grad = lax.psum((local_mat, local_vec), ('rows', 'blk'))  35 us
    psum x1, blocking collectives, local(): matrix_grad, vector_grad = lax.psum((local_mat, local_vec), ('rows', 'blk'))  28 us
    reduce_scatter x1, waiting for transfers between devices, local(): lax.psum_scatter(partial_out.astype(jnp.bfloat16), 'tp', scatter_dimensio...  26.3 us
    all_gather x1, blocking collectives, local(): lax.all_gather(keys_local, 'blk', axis=0, tiled=True)  18.3 us
    psum x2, blocking collectives, layer_stats(): center_mean = lax.psum(jnp.sum(hidden, 1), 'tp') / model_width  17.8 us
    psum x2, blocking collectives, norm_back(): lax.psum((jnp.sum(scaled, 1), jnp.sum(scaled * normed, 1)), 'tp')  17.7 us
    psum x2, blocking collectives, layer_stats(): variance = lax.psum(jnp.sum(centered * centered, 1), 'tp') / model_width  16.9 us
  transfers between devices with their start and end apart: 4, of which 4 were waited for; matrix products, arithmetic and copies ran while one was open for 2% of the time, Pallas kernels for 0%

commit v1 on v0

v1 whole, which is shorter than its diff:
```python
import math
from functools import partial

import jax
import jax.numpy as jnp
from jax import lax
from jax.experimental import pallas as pl
from jax.experimental.pallas import tpu as pltpu
from jax.sharding import PartitionSpec as P

HD = 64
HG = 768
MESH = pl.DeviceIdType.MESH
f32 = jnp.float32
bf16 = jnp.bfloat16

eps_norm = 1e-12
beta_one = 0.9
beta_two = 0.999
adam_eps = 1e-06
step_count = 100.0
decay_rate = 0.01
learn_rate = 0.04
matrix_rate = 1.0
NEG = -1e30


def nn(a, b):
    return jnp.dot(a, b, preferred_element_type=f32)


def nt(a, b, **kw):
    return lax.dot_general(a, b, (((1,), (1,)), ((), ())), preferred_element_type=f32, **kw)


def eye(n, dtype=bf16):
    rows = lax.broadcasted_iota(jnp.int32, (n, n), 0)
    cols = lax.broadcasted_iota(jnp.int32, (n, n), 1)
    return (rows == cols).astype(dtype)


def flip(a):
    return nt(eye(a.shape[1]), a)


def split_bf16(a):
    high = a.astype(bf16)
    return high, (a - high.astype(f32)).astype(bf16)


def lane_sums(a):
    return nt(jnp.ones((8, a.shape[1]), bf16), a)[0:1]


def lane_sums_f32(a):
    high, low = split_bf16(a)
    return lane_sums(high) + lane_sums(low)


def lamb_moments(gradient, first_moment, second_moment):
    first_new = beta_one * first_moment + (1.0 - beta_one) * gradient
    second_new = beta_two * second_moment + (1.0 - beta_two) * gradient * gradient
    update = (
        first_new
        / (1.0 - beta_one**step_count)
        / (jnp.sqrt(second_new / (1.0 - beta_two**step_count)) + adam_eps)
    )
    return first_new, second_new, update


def gelu_pair(pre):
    half = 0.5 * (1.0 + lax.erf(pre * (2.0**-0.5)))
    slope = half + pre * (jnp.exp(-0.5 * pre * pre) * ((2.0 * math.pi) ** -0.5))
    return pre * half, slope


class Sizes:
    def __init__(self, mesh_shape, tokens, row_count):
        self.nr = mesh_shape["rows"]
        self.nb = mesh_shape["blk"]
        self.nt = mesh_shape["tp"]
        self.t, self.g = tokens
        self.d = self.g * self.nt
        self.heads = self.g // HD
        self.row = row_count
        self.wide = self.heads * self.t
        self.half = HG // 2
        self.keep = self.nb <= 8
        owners = self.nb
        while self.nb % owners or self.g % (16 * owners):
            owners -= 1
        self.owners = owners
        self.rq = self.g // owners
        o = 3 * self.g
        self.lo = (o + self.d + HG, o + self.d, o, 0)
        self.width = (HG, HG, self.d, o)


def scratch_of(s):
    V = pltpu.VMEM
    D = pltpu.SemaphoreType.DMA
    T, G, nb, ntp = s.t, s.g, s.nb, s.nt
    kept = nb if s.keep else 1
    shapes = dict(
        xall=V((nb, T, G), bf16),
        xtall=V((kept, G, T), bf16),
        xtf=V((ntp, G, T), bf16),
        wot=V((ntp, s.d, G), bf16),
        vec=V((ntp, 16, G), f32),
        ctxg=V((ntp, G, T), bf16),
        st1=V((ntp, 8, T), f32),
        dmg=V((ntp, G, T), bf16),
        st2=V((ntp, 8, T), f32),
        nrm=V((ntp, 16, 128), f32),
        dxs=V((nb, T, G), bf16),
        dxr=V((nb, T, G), bf16),
        gsrc=V((4, 2, G, s.half), bf16),
        gcore=V((4, G, s.half), bf16),
        ghalf=V((4, s.owners, s.rq, s.half), bf16),
        gz=V((4, nb, s.rq, s.half), bf16),
        gfin=V((4, 2, s.owners, s.rq, s.half), bf16),
        vgl=V((16, G), f32),
        vgc=V((16, G), f32),
        vgs=V((16, G), f32),
        vgz=V((nb, 16, G), f32),
        mom=V((G, s.lo[0] + HG), f32),
        squ=V((G, s.lo[0] + HG), f32),
        wq_t=V((G, G), bf16),
        wk=V((G, G), bf16),
        wk_t=V((G, G), bf16),
        wv=V((G, G), bf16),
        wv_t=V((G, G), bf16),
        wo=V((G, s.d), bf16),
        w1=V((G, HG), bf16),
        w1_t=V((HG, G), bf16),
        w2=V((G, HG), bf16),
        w2_t=V((HG, G), bf16),
        qz=V((G, s.wide), bf16),
        dcz=V((G, s.wide), bf16),
        idk=V((kept, T, 128), f32),
        ebuf=V((kept, T, s.wide), bf16),
        mrec=V((nb, 1, s.wide), f32),
        mrun=V((1, s.wide), f32),
        lrun=V((1, s.wide), f32),
        acc=V((G, T), f32),
        delta=V((1, s.wide), f32),
        lse=V((1, s.wide), f32),
        n1f=V((ntp, G, T), f32),
        datt=V((s.d, T), bf16),
        act=V((HG, T), bf16),
        slope=V((HG, T), f32),
        mid=V((G, T), f32),
        dqt=V((G, T), f32),
        gkv=V((2, G, G), f32),
        dsb=V((T, s.wide), bf16),
        pb=V((T, s.wide), bf16),
        vb=V((1, G), f32),
        dxo=V((T, G), f32),
        x_s=D((nb,)), x_r=D((nb,)),
        xt_s=D((ntp,)), xt_r=D((ntp,)),
        wo_s=D((ntp,)), wo_r=D((ntp,)),
        vec_s=D((ntp,)), vec_r=D((ntp,)),
        ctx_s=D((ntp,)), ctx_r=D((ntp,)),
        st1_s=D((ntp,)), st1_r=D((ntp,)),
        dmg_s=D((ntp,)), dmg_r=D((ntp,)),
        st2_s=D((ntp,)), st2_r=D((ntp,)),
        nrm_s=D((ntp,)), nrm_r=D((ntp,)),
        dx_s=D((nb,)), dx_r=D((nb,)),
        gc_s=D((4,)), gc_r=D((4,)),
        gz_s=D((4, nb)), gz_r=D((4, nb)),
        ga_s=D((4, nb)), ga_r=D((4, nb)),
        gd_s=D((4,)), gd_r=D((4,)),
        vc_s=D((1,)), vc_r=D((1,)),
        vz_s=D((nb,)), vz_r=D((nb,)),
        loc=D((2,)),
    )
    return list(shapes.keys()), list(shapes.values())


def layer_kernel(s, names, x_ref, cot_ref, ids_ref, w_ref, v_ref, mom_hbm, squ_hbm,
                 out_ref, ig_ref, g_ref, vg_ref, ratio_ref, *scratch):
    r = dict(zip(names, scratch))
    T, G, nb, ntp = s.t, s.g, s.nb, s.nt
    c, b, t = lax.axis_index("rows"), lax.axis_index("blk"), lax.axis_index("tp")
    core = (1 - c, b, t)
    tx, ty = t % 2, t // 2
    tp_peers = [ty * 2 + (1 - tx), (1 - ty) * 2 + tx, 3 - t]
    z_peers = [(b + o) % nb for o in range(1, nb)]

    def tp_dev(k):
        return (c, b, k)

    def z_dev(k):
        return (c, k, t)

    sent = []

    def copy(src, dst, ssem, rsem, dev):
        return pltpu.make_async_remote_copy(
            src_ref=src, dst_ref=dst, send_sem=ssem, recv_sem=rsem, device_id=dev, device_id_type=MESH
        )

    def push(src, dst, ssem, rsem, dev):
        one = copy(src, dst, ssem, rsem, dev)
        one.start()
        sent.append(one)

    def arrive(dst, ssem, rsem, dev):
        copy(dst, dst, ssem, rsem, dev).wait_recv()

    def tp_push(name):
        for k in tp_peers:
            push(r[name].at[t], r[name].at[t], r[SEM[name] + "_s"].at[k],
                 r[SEM[name] + "_r"].at[t], tp_dev(k))

    def tp_wait(name, k):
        arrive(r[name].at[k], r[SEM[name] + "_s"].at[k], r[SEM[name] + "_r"].at[k], tp_dev(k))

    SEM = dict(xtf="xt", wot="wo", vec="vec", ctxg="ctx", st1="st1", dmg="dmg", st2="st2", nrm="nrm")

    barrier = pltpu.get_barrier_semaphore()
    pl.semaphore_signal(barrier, 1, device_id=core, device_id_type=MESH)
    for k in tp_peers:
        pl.semaphore_signal(barrier, 1, device_id=tp_dev(k), device_id_type=MESH)
    for k in z_peers:
        pl.semaphore_signal(barrier, 1, device_id=z_dev(k), device_id_type=MESH)
    local_m = pltpu.make_async_copy(mom_hbm, r["mom"], r["loc"].at[0])
    local_s = pltpu.make_async_copy(squ_hbm, r["squ"], r["loc"].at[1])
    local_m.start()
    local_s.start()

    x_own = x_ref[...]
    r["xall"][b] = x_own
    x_t = flip(x_own).astype(bf16)
    if s.keep:
        r["xtall"][b] = x_t
    r["xtf"][t] = x_t
    r["vec"][t, 0:12, :] = v_ref[...]
    r["vec"][t, 12:16, :] = jnp.zeros((4, G), f32)
    w_o = w_ref[:, s.lo[2]:s.lo[2] + s.d].astype(bf16)
    r["wo"][...] = w_o
    r["wot"][t] = flip(w_o).astype(bf16)
    pl.semaphore_wait(barrier, 1 + (ntp - 1) + (nb - 1))

    for k in z_peers:
        push(r["xall"].at[b], r["xall"].at[b], r["x_s"].at[k], r["x_r"].at[b], z_dev(k))
    tp_push("vec")
    tp_push("xtf")
    tp_push("wot")

    w_q = w_ref[:, 0:G].astype(bf16)
    w_k = w_ref[:, G:2 * G].astype(bf16)
    w_v = w_ref[:, 2 * G:3 * G].astype(bf16)
    r["wq_t"][...] = flip(w_q).astype(bf16)
    r["wk"][...] = w_k
    r["wk_t"][...] = flip(w_k).astype(bf16)
    r["wv"][...] = w_v
    r["wv_t"][...] = flip(w_v).astype(bf16)
    w_1 = w_ref[:, s.lo[1]:s.lo[1] + HG].astype(bf16)
    w_2 = w_ref[:, s.lo[0]:s.lo[0] + HG].astype(bf16)
    r["w1"][...] = w_1
    r["w1_t"][...] = flip(w_1).astype(bf16)
    r["w2"][...] = w_2
    r["w2_t"][...] = flip(w_2).astype(bf16)

    def columns_of(vec):
        return nt(eye(G, f32), vec, precision=lax.Precision.HIGHEST)

    v_cols = columns_of(r["vec"][t])

    def v_col(k):
        return v_cols[:, k:k + 1]

    bias_v_row = v_ref[1:2, :]
    bias_v_col = v_col(1)

    scaling = HD**-0.5
    q_t = (nt(r["wq_t"][...], x_own) + v_col(0)).astype(bf16)
    q_t = (q_t.astype(f32) * scaling)
    head_of = lax.broadcasted_iota(jnp.int32, (G, T), 0) // HD

    def by_head(a):
        return [jnp.where(head_of == h, a, 0.0).astype(bf16) for h in range(s.heads)]

    for h, part in enumerate(by_head(q_t)):
        r["qz"][:, h * T:(h + 1) * T] = part

    def ids_of(j):
        return ids_ref[:, pl.ds(pl.multiple_of(j * T, 128), T)].astype(f32)

    def id_columns(j):
        ids = ids_of(j)
        high = jnp.floor(ids * (1.0 / 128.0))
        low = ids - 128.0 * high
        high, low = (jnp.broadcast_to(a, (128, T)).astype(bf16) for a in (high, low))
        return 128.0 * nt(eye(T), high) + nt(eye(T), low)

    if s.keep:
        for k in range(nb):
            r["idk"][k] = id_columns(k)
    id_q = ids_of(b)

    r["mrun"][...] = jnp.full((1, s.wide), NEG, f32)
    r["lrun"][...] = jnp.zeros((1, s.wide), f32)
    r["acc"][...] = jnp.zeros((G, T), f32)

    def same_doc(j):
        keys = r["idk"][j] if s.keep else id_columns(j)
        return jnp.concatenate([keys] * (T // 128), axis=1) == id_q

    def forward_block(j):
        x_j = r["xall"][j]
        keys = nn(x_j, r["wk"][...]).astype(bf16)
        vals_t = (nt(r["wv_t"][...], x_j) + bias_v_col).astype(bf16)
        mask = same_doc(j)
        for h in range(s.heads):
            cols = slice(h * T, (h + 1) * T)
            rows = slice(h * HD, (h + 1) * HD)
            score = jnp.where(mask, nn(keys, r["qz"][:, cols]), NEG)
            old = r["mrun"][:, cols]
            top = jnp.maximum(old, jnp.max(score, axis=0, keepdims=True))
            fade = jnp.exp(old - top)
            e = jnp.exp(score - top)
            r["lrun"][:, cols] = r["lrun"][:, cols] * fade + jnp.sum(e, axis=0, keepdims=True)
            e = e.astype(bf16)
            if s.keep:
                r["ebuf"][j, :, cols] = e
                r["mrec"][j, :, cols] = top
            r["mrun"][:, cols] = top
            r["acc"][rows, :] = r["acc"][rows, :] * fade + nn(vals_t[rows, :], e)

    forward_block(b)

    def forward_remote(o):
        j = (b + o) % nb
        arrive(r["xall"].at[j], r["x_s"].at[j], r["x_r"].at[j], z_dev(j))
        if s.keep:
            r["xtall"][j] = flip(r["xall"][j]).astype(bf16)
        forward_block(j)

    def each_remote(body):
        if nb <= 4:
            for o in range(1, nb):
                body(o)
        else:
            lax.fori_loop(1, nb, lambda o, _: (body(o), 0)[1], 0)

    each_remote(forward_remote)

    r["lse"][...] = r["mrun"][...] + jnp.log(r["lrun"][...])
    context = jnp.concatenate(
        [
            r["acc"][h * HD:(h + 1) * HD, :] / r["lrun"][:, h * T:(h + 1) * T]
            for h in range(s.heads)
        ],
        axis=0,
    )
    r["acc"][...] = context
    r["ctxg"][t] = context.astype(bf16)
    tp_push("ctxg")

    for k in tp_peers:
        tp_wait("vec", k)
        tp_wait("xtf", k)
        tp_wait("wot", k)
    att = nn(r["wot"][t], r["ctxg"][t])
    for k in tp_peers:
        tp_wait("ctxg", k)
        att = att + nn(r["wot"][k], r["ctxg"][k])
    hidden = []
    for k in range(ntp):
        bias = columns_of(r["vec"][k])[:, 2:3]
        hidden.append(r["xtf"][k].astype(f32) + att[k * G:(k + 1) * G] + bias)
    mean1 = sum(jnp.sum(a, axis=0, keepdims=True) for a in hidden) / s.d
    hidden = [a - mean1 for a in hidden]
    var1 = sum(jnp.sum(a * a, axis=0, keepdims=True) for a in hidden) / s.d
    inv1 = lax.rsqrt(var1 + eps_norm)
    for k in range(ntp):
        r["n1f"][k] = hidden[k] * inv1
    gain1 = v_col(3)
    mid = r["n1f"][t] * gain1 + v_col(4)
    mid_low = mid.astype(bf16)
    r["mid"][...] = mid

    bias_rows = HG // G
    hid_bias = jnp.concatenate([v_col(5 + k) for k in range(bias_rows)], axis=0)
    pre = nn(r["w1_t"][...], mid_low) + hid_bias
    act, slope = gelu_pair(pre)
    r["act"][...] = act.astype(bf16)
    r["slope"][...] = slope
    h2 = mid + nn(r["w2"][...], r["act"][...]) + v_col(5 + bias_rows)
    gain2 = v_col(6 + bias_rows)
    shift2 = v_col(7 + bias_rows)
    cot = flip(cot_ref[...])
    scaled = cot * gain2
    sum1 = jnp.sum(h2, axis=0, keepdims=True)
    h2c = h2 - sum1 / G
    sum2 = jnp.sum(h2c * h2c, axis=0, keepdims=True)
    sum3 = jnp.sum(scaled, axis=0, keepdims=True)
    sum4 = jnp.sum(scaled * h2c, axis=0, keepdims=True)
    r["st1"][t] = jnp.concatenate([sum1, sum2, sum3, sum4, jnp.zeros((4, T), f32)], axis=0)
    tp_push("st1")
    for k in tp_peers:
        tp_wait("st1", k)
    stats = [r["st1"][k] for k in range(ntp)]
    mean2 = sum(a[0:1] for a in stats) / s.d
    offs = [a[0:1] / G - mean2 for a in stats]
    var2 = sum(a[1:2] + G * o * o for a, o in zip(stats, offs)) / s.d
    inv2 = lax.rsqrt(var2 + eps_norm)
    first = sum(a[2:3] for a in stats) / s.d
    second = sum(a[3:4] + a[2:3] * o for a, o in zip(stats, offs)) * inv2 / s.d
    n2 = (h2 - mean2) * inv2
    out_ref[...] = nt(eye(T), (n2 * gain2 + shift2).astype(bf16)).astype(bf16)
    d2 = inv2 * (scaled - first - n2 * second)
    dffn = d2.astype(bf16)
    dact = nn(r["w2_t"][...], dffn)
    dpre = (dact * r["slope"][...]).astype(bf16)
    dmid = d2 + nn(r["w1"][...], dpre)
    n1 = r["n1f"][t]
    dmg = dmid * gain1
    part1 = jnp.sum(dmg, axis=0, keepdims=True)
    part2 = jnp.sum(dmg * n1, axis=0, keepdims=True)
    r["st2"][t] = jnp.concatenate([part1, part2, jnp.zeros((6, T), f32)], axis=0)
    r["dmg"][t] = dmg.astype(bf16)
    tp_push("st2")
    tp_push("dmg")

    def sum_start(m):
        push(r["gsrc"].at[m, 1 - c], r["gcore"].at[m], r["gc_s"].at[m], r["gc_r"].at[m], core)

    def sum_spread(m):
        arrive(r["gcore"].at[m], r["gc_s"].at[m], r["gc_r"].at[m], core)
        both = (r["gsrc"][m, c].astype(f32) + r["gcore"][m].astype(f32)).astype(bf16)
        for k in range(s.owners):
            r["ghalf"][m, k] = both[k * s.rq:(k + 1) * s.rq]

        def to_owner(j):
            push_or = copy(r["ghalf"].at[m, j], r["gz"].at[m, b], r["gz_s"].at[m, j], r["gz_r"].at[m, b], z_dev(j))
            push_or.start()

        for j in z_peers:
            if s.owners < nb:
                pl.when(j < s.owners)(partial(to_owner, j))
            else:
                to_owner(j)

    def owner_only(body):
        if s.owners < nb:
            pl.when(b < s.owners)(body)
        else:
            body()

    def sum_own(m):
        def body():
            for j in z_peers:
                arrive(r["gz"].at[m, j], r["gz_s"].at[m, 0], r["gz_r"].at[m, j], z_dev(j))
            r["gz"][m, b] = r["ghalf"][m, b]
            total = r["gz"][m, 0].astype(f32)
            for j in range(1, nb):
                total = total + r["gz"][m, j].astype(f32)
            r["gfin"][m, c, b] = total.astype(bf16)
            for j in z_peers:
                copy(r["gfin"].at[m, c, b], r["gfin"].at[m, c, b], r["ga_s"].at[m, j], r["ga_r"].at[m, b], z_dev(j)).start()

        owner_only(body)

    def sum_share(m):
        for j in z_peers:
            def got(j=j):
                arrive(r["gfin"].at[m, c, j], r["ga_s"].at[m, 0], r["ga_r"].at[m, j], z_dev(j))
            if s.owners < nb:
                pl.when(j < s.owners)(got)
            else:
                got()
        push(r["gfin"].at[m, c], r["gfin"].at[m, c], r["gd_s"].at[m], r["gd_r"].at[m], core)

    def sum_done(m):
        arrive(r["gfin"].at[m, 1 - c], r["gd_s"].at[m], r["gd_r"].at[m], core)

    def sum_sends_done(m):
        for j in z_peers:
            def done(j=j):
                copy(r["ghalf"].at[m, j], r["gz"].at[m, b], r["gz_s"].at[m, j], r["gz_r"].at[m, b], z_dev(j)).wait_send()
            if s.owners < nb:
                pl.when(j < s.owners)(done)
            else:
                done()

        def body():
            for j in z_peers:
                copy(r["gfin"].at[m, c, b], r["gfin"].at[m, c, b], r["ga_s"].at[m, j], r["ga_r"].at[m, b], z_dev(j)).wait_send()

        owner_only(body)

    def keep_grad(m, grad):
        r["gsrc"][m, 0] = grad[:, 0:s.half].astype(bf16)
        r["gsrc"][m, 1] = grad[:, s.half:].astype(bf16)

    keep_grad(0, nt(dffn, r["act"][...]))
    sum_start(0)
    keep_grad(1, nt(mid_low, dpre))
    sum_start(1)
    vgl = r["vgl"]
    vgl[12:16, :] = jnp.zeros((4, G), f32)
    vgl[3:4, :] = lane_sums_f32(dmid * n1)
    vgl[4:5, :] = lane_sums_f32(dmid)
    hid_sum = lane_sums(dpre)
    for k in range(bias_rows):
        vgl[5 + k:6 + k, :] = hid_sum[:, k * G:(k + 1) * G]
    vgl[5 + bias_rows:6 + bias_rows, :] = lane_sums(dffn)
    vgl[6 + bias_rows:7 + bias_rows, :] = lane_sums_f32(cot * n2)
    vgl[7 + bias_rows:8 + bias_rows, :] = lane_sums_f32(cot)

    for k in tp_peers:
        tp_wait("st2", k)
    stats = [r["st2"][k] for k in range(ntp)]
    first = sum(a[0:1] for a in stats) / s.d
    second = sum(a[1:2] for a in stats) / s.d
    d1_own = inv1 * (dmg - first - n1 * second)
    for k in tp_peers:
        tp_wait("dmg", k)
    for k in range(ntp):
        part = inv1 * (r["dmg"][k].astype(f32) - first - r["n1f"][k] * second)
        r["datt"][k * G:(k + 1) * G, :] = part.astype(bf16)
    vgl[2:3, :] = lane_sums(d1_own.astype(bf16))
    dctx = nn(r["wo"][...], r["datt"][...]).astype(bf16).astype(f32)
    for h, part in enumerate(by_head(dctx)):
        r["dcz"][:, h * T:(h + 1) * T] = part
        rows = slice(h * HD, (h + 1) * HD)
        r["delta"][:, h * T:(h + 1) * T] = jnp.sum(dctx[rows] * r["acc"][rows, :], axis=0, keepdims=True)
    sum_spread(0)
    sum_spread(1)
    keep_grad(2, nt(r["ctxg"][t], r["datt"][...]))
    sum_start(2)
    d1_high, d1_low = split_bf16(d1_own)
    r["dxo"][...] = nt(eye(T), d1_high) + nt(eye(T), d1_low)

    r["dqt"][...] = jnp.zeros((G, T), f32)
    r["gkv"][...] = jnp.zeros((2, G, G), f32)
    r["vb"][...] = jnp.zeros((1, G), f32)

    def backward_block(j):
        x_j = r["xall"][j]
        keys_t = nt(r["wk_t"][...], x_j).astype(bf16)
        vals = (nn(x_j, r["wv"][...]) + bias_v_row).astype(bf16)
        if not s.keep:
            keys = nn(x_j, r["wk"][...]).astype(bf16)
            mask = same_doc(j)
        for h in range(s.heads):
            cols = slice(h * T, (h + 1) * T)
            rows = slice(h * HD, (h + 1) * HD)
            if s.keep:
                weight = jnp.exp(r["mrec"][j, :, cols] - r["lse"][:, cols])
                p = r["ebuf"][j, :, cols].astype(f32) * weight
            else:
                p = jnp.exp(jnp.where(mask, nn(keys, r["qz"][:, cols]), NEG) - r["lse"][:, cols])
            dp = nn(vals, r["dcz"][:, cols])
            ds = (p * (dp - r["delta"][:, cols])).astype(bf16)
            r["dsb"][:, cols] = ds
            r["pb"][:, cols] = p.astype(bf16)
            r["dqt"][rows, :] += nn(keys_t[rows, :], ds)
        dk = nt(r["dsb"][...], r["qz"][...]).astype(bf16)
        dv = nt(r["pb"][...], r["dcz"][...]).astype(bf16)
        x_jt = r["xtall"][j] if s.keep else flip(x_j).astype(bf16)
        r["gkv"][0] += nn(x_jt, dk)
        r["gkv"][1] += nn(x_jt, dv)
        r["vb"][...] += jnp.sum(dv.astype(f32), axis=0, keepdims=True)
        return nn(dk, r["wk_t"][...]) + nn(dv, r["wv_t"][...])

    def backward_remote(o):
        j = (b + o) % nb
        r["dxs"][j] = backward_block(j).astype(bf16)
        copy(r["dxs"].at[j], r["dxr"].at[b], r["dx_s"].at[j], r["dx_r"].at[b], z_dev(j)).start()
        if nb <= 4:
            stages = {1: (sum_own, 0, 1), 2: (sum_share, 0, 1), 3: (sum_spread, 2)}
            if o in stages:
                for m in stages[o][1:]:
                    stages[o][0](m)

    each_remote(backward_remote)
    if nb < 4 or nb > 4:
        sum_own(0)
        sum_own(1)
        sum_share(0)
        sum_share(1)
        sum_spread(2)
    dx = backward_block(b)
    dq_t = (r["dqt"][...] * scaling).astype(bf16)
    r["gsrc"][3, 0, :, 0:G] = nt(r["xtall"][b], dq_t).astype(bf16)
    r["gsrc"][3, 0, :, G:2 * G] = r["gkv"][0].astype(bf16)
    r["gsrc"][3, 1, :, 0:G] = r["gkv"][1].astype(bf16)
    r["gsrc"][3, 1, :, G:2 * G] = jnp.zeros((G, G), bf16)
    sum_start(3)
    vgl[0:1, :] = lane_sums(dq_t)
    vgl[1:2, :] = r["vb"][...]
    push(vgl, r["vgc"], r["vc_s"].at[0], r["vc_r"].at[0], core)
    r["dxo"][...] += dx + nn(nt(eye(T), dq_t).astype(bf16), r["wq_t"][...])
    sum_own(2)
    sum_spread(3)
    arrive(r["vgc"], r["vc_s"].at[0], r["vc_r"].at[0], core)
    r["vgs"][...] = vgl[...] + r["vgc"][...]
    r["vgz"][b] = r["vgs"][...]
    for j in z_peers:
        push(r["vgs"], r["vgz"].at[b], r["vz_s"].at[j], r["vz_r"].at[b], z_dev(j))
    sum_share(2)
    local_m.wait()
    local_s.wait()

    def norms_of(m):
        rows = []
        for h in range(2):
            lo = s.lo[m] + h * s.half
            wide = min(s.half, s.lo[m] + s.width[m] - lo)
            grad = jnp.concatenate([r["gfin"][m, h, k] for k in range(s.owners)], axis=0)[:, :wide]
            w = w_ref[:, lo:lo + wide]
            _, _, u = lamb_moments(grad.astype(f32), r["mom"][:, lo:lo + wide], r["squ"][:, lo:lo + wide])
            u = u + decay_rate * w
            rows.append((jnp.sum(w * w, axis=0, keepdims=True), jnp.sum(u * u, axis=0, keepdims=True)))
        return rows

    def total(a):
        return jnp.broadcast_to(jnp.sum(a, axis=1, keepdims=True), (1, 128))

    sums = {}
    for m in (0, 1):
        sum_done(m)
        sums[m] = norms_of(m)
    sum_own(3)
    sum_done(2)
    sums[2] = norms_of(2)
    for j in z_peers:
        arrive(r["dxr"].at[j], r["dx_s"].at[j], r["dx_r"].at[j], z_dev(j))
    got = r["dxo"][...]
    for j in z_peers:
        got = got + r["dxr"][j].astype(f32)
    ig_ref[...] = got
    sum_share(3)
    for j in z_peers:
        arrive(r["vgz"].at[j], r["vz_s"].at[j], r["vz_r"].at[j], z_dev(j))
    vg = r["vgz"][0]
    for j in range(1, nb):
        vg = vg + r["vgz"][j]
    vg_ref[...] = vg[0:12]
    sum_done(3)
    sums[3] = norms_of(3)
    packed = []
    for which in range(2):
        lead = sums[3][0][which]
        packed += [total(lead[:, 0:G]), total(lead[:, G:2 * G]), total(sums[3][1][which])]
        packed += [total(sums[m][0][which] + sums[m][1][which]) for m in (2, 1, 0)]
        packed += [jnp.zeros((2, 128), f32)]
    r["nrm"][t] = jnp.concatenate(packed, axis=0)
    tp_push("nrm")
    for m in range(4):
        for h in range(2):
            for k in range(s.owners):
                g_ref[m, h, k] = r["gfin"][m, h, k]
    for k in tp_peers:
        tp_wait("nrm", k)
    norms = r["nrm"][0]
    for k in range(1, ntp):
        norms = norms + r["nrm"][k]
    ratio_ref[...] = jnp.sqrt(norms[0:8] / (norms[8:16] + 1e-12))

    for one in sent:
        one.wait_send()
    for m in range(4):
        sum_sends_done(m)
    for j in z_peers:
        copy(r["dxs"].at[j], r["dxr"].at[b], r["dx_s"].at[j], r["dx_r"].at[b], z_dev(j)).wait_send()


def finish_kernel(s, out_in, ig_in, w_ref, mom_ref, squ_ref, g_ref, ratio_ref, v_ref, vg_ref, mv_ref, sv_ref,
                  out_ref, ig_ref, gm_ref, gv_ref, nm_ref, ns_ref, nmv_ref, nsv_ref, nw_ref, nv_ref, grad):
    out_ref[...] = out_in[...]
    ig_ref[...] = ig_in[...]
    for m in range(4):
        for h in range(2):
            lo = s.lo[m] + h * s.half
            wide = min(s.half, s.lo[m] + s.width[m] - lo)
            grad[:, lo:lo + wide] = g_ref[m, h, 0, :, 0:wide].astype(f32)
    cols = s.lo[0] + HG
    g = grad[:, 0:cols]
    gm_ref[...] = g
    new_m, new_s, u = lamb_moments(g, mom_ref[...], squ_ref[...])
    nm_ref[...] = new_m
    ns_ref[...] = new_s
    w = w_ref[...]
    u = u + decay_rate * w
    col = lax.broadcasted_iota(jnp.int32, (1, cols), 1)
    ratio = jnp.broadcast_to(ratio_ref[5:6, 0:1], (1, cols))
    for k, edge in ((4, s.lo[0]), (3, s.lo[1]), (2, s.lo[2]), (1, 2 * s.g), (0, s.g)):
        ratio = jnp.where(col < edge, ratio_ref[k:k + 1, 0:1], ratio)
    nw_ref[...] = w - matrix_rate * ratio * u

    @pl.when(pl.program_id(0) == 0)
    def _():
        vg = vg_ref[...]
        gv_ref[...] = vg
        new_mv, new_sv, uv = lamb_moments(vg, mv_ref[...], sv_ref[...])
        nmv_ref[...] = new_mv
        nsv_ref[...] = new_sv
        nv_ref[...] = v_ref[...] - learn_rate * uv


def local(mesh_shape, tokens, cotangent, segment_ids, matrices, vectors, moment_mat, square_mat, moment_vec, square_vec):
    s = Sizes(mesh_shape, tokens.shape, segment_ids.shape[1])
    names, scratch = scratch_of(s)
    vmem = pl.BlockSpec(memory_space=pltpu.VMEM)
    S = jax.ShapeDtypeStruct
    output, input_grad, grads, vector_grad, ratio = pl.pallas_call(
        partial(layer_kernel, s, names),
        out_shape=(
            S(tokens.shape, bf16),
            S(tokens.shape, f32),
            S((4, 2, s.owners, s.rq, s.half), bf16),
            S(vectors.shape, f32),
            S((8, 128), f32),
        ),
        in_specs=[vmem] * 5 + [pl.BlockSpec(memory_space=pl.ANY)] * 2,
        out_specs=(vmem,) * 5,
        scratch_shapes=scratch,
        compiler_params=pltpu.CompilerParams(
            collective_id=0, has_side_effects=True, vmem_limit_bytes=60 * 2**20
        ),
        name="layer",
    )(tokens, cotangent, segment_ids, matrices, vectors, moment_mat, square_mat)

    steps = s.owners
    tok = s.t // steps

    def rows(a, n):
        return pl.BlockSpec((n, a.shape[1]), lambda i: (i, 0))

    def whole(a):
        return pl.BlockSpec(a.shape, lambda i: (0, 0))

    mat = rows(matrices, s.rq)
    vec = whole(vectors)
    return pl.pallas_call(
        partial(finish_kernel, s),
        grid=(steps,),
        out_shape=(
            S(tokens.shape, bf16),
            S(tokens.shape, f32),
            S(matrices.shape, f32),
            S(vectors.shape, f32),
            S(matrices.shape, f32),
            S(matrices.shape, f32),
            S(vectors.shape, f32),
            S(vectors.shape, f32),
            S(matrices.shape, f32),
            S(vectors.shape, f32),
        ),
        in_specs=[
            rows(tokens, tok), rows(tokens, tok), mat, mat, mat,
            pl.BlockSpec((4, 2, 1, s.rq, s.half), lambda i: (0, 0, i, 0, 0)),
            pl.BlockSpec((8, 128), lambda i: (0, 0)), vec, vec, vec, vec,
        ],
        out_specs=(rows(tokens, tok), rows(tokens, tok), mat, vec, mat, mat, vec, vec, mat, vec),
        scratch_shapes=[pltpu.VMEM((s.rq, s.lo[0] + HG), f32)],
        compiler_params=pltpu.CompilerParams(vmem_limit_bytes=40 * 2**20),
        name="finish",
    )(output, input_grad, matrices, moment_mat, square_mat, grads, ratio, vectors, vector_grad, moment_vec, square_vec)


def solution(mesh):
    return jax.shard_map(
        partial(local, dict(mesh.shape)),
        mesh=mesh,
        in_specs=(
            P(("rows", "blk"), "tp"),
            P(("rows", "blk"), "tp"),
            P("rows", None),
            P("tp", None),
            P(None, "tp"),
            P("tp", None),
            P("tp", None),
            P(None, "tp"),
            P(None, "tp"),
        ),
        out_specs=(
            P(("rows", "blk"), "tp"),
            P(("rows", "blk"), "tp"),
            P("tp", None),
            P(None, "tp"),
            P("tp", None),
            P("tp", None),
            P(None, "tp"),
            P(None, "tp"),
            P("tp", None),
            P(None, "tp"),
        ),
        check_vma=False,
    )
```

time: 335 us -> 127 us (0.38)
  blocking collectives: 135 us -> 0 us
  Pallas kernels: 0 us -> 113 us
  waiting for transfers between devices: 106 us -> 0 us
  matrix products: 32.2 us -> 0 us
  other arithmetic: 24 us -> 0 us
  between operations: 14.3 us -> 0.7 us
  local copies, waits for them, and re-layouts: 21.7 us -> 13 us
    pallas_call x0 -> x2, Pallas kernels: none -> 113 us  [the longest x1 108 us: local(): pl.pallas_call(partial(layer_kernel, s, names), out_shape=(S(tokens.shape...]
    psum x8 -> x0, blocking collectives: 90.3 us -> none  [the longest x1 28 us: local(): matrix_grad, vector_grad = lax.psum((local_mat, local_vec), ('rows', 'blk'))]
    unnamed x6 -> x0, waiting for transfers between devices: 45.2 us -> none
    all_gather x3 -> x0, blocking collectives: 44.5 us -> none  [the longest x1 18.3 us: local(): lax.all_gather(keys_local, 'blk', axis=0, tiled=True)]
    psum x1 -> x0, waiting for transfers between devices: 35 us -> none  [local(): matrix_grad, vector_grad = lax.psum((local_mat, local_vec), ('rows', 'blk'))]
    dot_general x33 -> x0, matrix products: 32.2 us -> none  [the longest x1 5.28 us: local(): jnp.dot(middle_low, w_hidden, preferred_element_type=f32)]
    reduce_scatter x1 -> x0, waiting for transfers between devices: 26.3 us -> none  [local(): lax.psum_scatter(partial_out.astype(jnp.bfloat16), 'tp', scatter_dimensio...]
    reduce_sum x10 -> x0, other arithmetic: 12.5 us -> none  [the longest x1 7 us: local(): update_cols = jnp.sum(update_mat * update_mat, 0)]
  transfers between devices with their start and end apart: 4 -> 0, of which waited for: 4 -> 0; matrix products, arithmetic and copies ran while one was open for 2% -> 0% of each run, Pallas kernels for 0% -> 0%
where the time goes in v1:
time: 127 us; the launch traced here: 126 us
  Pallas kernels  113 us (89%)
  local copies, waits for them, and re-layouts  13 us (10%)
    pallas_call x1, Pallas kernels, local(): pl.pallas_call(partial(layer_kernel, s, names), out_shape=(S(tokens.shape...  108 us
    unnamed x24, local copies, waits for them, and re-layouts  11.3 us
    pallas_call x1, Pallas kernels, local(): pl.pallas_call(partial(finish_kernel, s), grid=(steps,), out_shape=(S(tok...  4.83 us

profile of v1, /device:TPU:0, one launch (start us, length us, event | category | flops | bytes accessed | tf_op | source)
XLA Modules:
  0.0 126.4 jit_solution(11833374196309124696)
XLA Ops:
  0.6 1.7 %copy.19.x_ref = bf16[384,192]{1,0:T(8,128)(2,1)} copy(bf16[384,192]{0,1:T(8,128)(2,1)} %param.9) | data formatting | bytes 294912 | tf_op args[0]
  2.4 1.7 %copy.20.cot_ref = bf16[384,192]{1,0:T(8,128)(2,1)} copy(bf16[384,192]{0,1:T(8,128)(2,1)} %param.10) | data formatting | bytes 294912 | tf_op args[1]
  4.1 0.0 copy-start
  4.1 0.0 copy-start.6
  4.1 0.0 copy-start.7
  4.1 0.0 copy-start.8
  4.1 107.9 %layer.1 = (bf16[384,192]{1,0:T(8,128)(2,1)}, f32[384,192]{1,0:T(8,128)}, bf16[4,2,4,48,384]{4,3,2,1,0:T(8,128)(2,1)}, f32[12,192]{1,0:T(8,128)}, f32[8,128]{1,0:T(8,128)}) custom-call(bf16[384,192]{1,0:T(8,128)(2,1)} %copy.19.x_ref, bf16[384,192]{1,0:T(8,128)(2,1)} %copy.20.cot_ref, s32[1,1536]{1,0:T(1,128)} %ids_ref.1, f32[192,2880]{1,0:T(8,128)} %w_ref.3, ...), custom_call_target="tpu_custom_call" | custom-call | tf_op jit(solution)/shard_map/layer/pallas_call | solution.py:711
  112.0 0.0 copy-done
  112.0 0.0 copy-done.6
  112.0 0.0 copy-done.7
  112.0 0.0 copy-done.8
  112.0 0.0 copy-start.1
  112.0 1.6 %copy-done.1 = f32[192,2880]{1,0:T(8,128)S(1)} copy-done((f32[192,2880]{1,0:T(8,128)S(1)}, f32[192,2880]{1,0:T(8,128)}, u32[]{:S(2)}) %copy-start.1) | copy-done | bytes 2211864
  113.7 0.0 copy-start.2
  113.7 1.6 %copy-done.2 = f32[192,2880]{1,0:T(8,128)S(1)} copy-done((f32[192,2880]{1,0:T(8,128)S(1)}, f32[192,2880]{1,0:T(8,128)}, u32[]{:S(2)}) %copy-start.2) | copy-done | bytes 2211864
  115.3 0.0 copy-start.3
  115.3 1.3 %copy-done.3 = bf16[4,2,4,48,384]{4,3,2,1,0:T(8,128)(2,1)S(1)} copy-done((bf16[4,2,4,48,384]{4,3,2,1,0:T(8,128)(2,1)S(1)}, bf16[4,2,4,48,384]{4,3,2,1,0:T(8,128)(2,1)}, u32[]{:S(2)}) %copy-start.3) | copy-done | bytes 1179672
  116.6 1.0 copy-done.4
  117.6 0.9 copy-done.5
  118.5 0.7 copy-done.9
  119.2 0.7 copy-done.10
  119.9 4.8 %finish.1 = (bf16[384,192]{1,0:T(8,128)(2,1)S(1)}, f32[384,192]{1,0:T(8,128)S(1)}, f32[192,2880]{1,0:T(8,128)}, f32[12,192]{1,0:T(8,128)}, f32[192,2880]{1,0:T(8...) custom-call(bf16[384,192]{1,0:T(8,128)(2,1)S(1)} %copy-done.5, ...), custom_call_target="tpu_custom_call" | custom-call | tf_op jit(solution)/shard_map/finish/pallas_call | solution.py:740
  124.7 0.8 copy.21
  125.5 0.9 copy.22
  (4 shorter events, 0.0 us)
Async XLA Ops:
  4.1 107.9 %copy-start = (f32[192,2880]{1,0:T(8,128)S(1)}, f32[192,2880]{1,0:T(8,128)}, u32[]{:S(2)}) copy-start(f32[192,2880]{1,0:T(8,128)} %w_ref.3) | copy-start | bytes 6635524
  4.1 107.9 %copy-start.6 = (f32[12,192]{1,0:T(8,128)S(1)}, f32[12,192]{1,0:T(8,128)}, u32[]{:S(2)}) copy-start(f32[12,192]{1,0:T(8,128)} %v_ref.3) | copy-start | bytes 27652
  4.1 107.9 %copy-start.7 = (f32[12,192]{1,0:T(8,128)S(1)}, f32[12,192]{1,0:T(8,128)}, u32[]{:S(2)}) copy-start(f32[12,192]{1,0:T(8,128)} %mv_ref.1) | copy-start | bytes 27652
  4.1 107.9 %copy-start.8 = (f32[12,192]{1,0:T(8,128)S(1)}, f32[12,192]{1,0:T(8,128)}, u32[]{:S(2)}) copy-start(f32[12,192]{1,0:T(8,128)} %sv_ref.1) | copy-start | bytes 27652
  112.0 1.6 %copy-start.1 = (f32[192,2880]{1,0:T(8,128)S(1)}, f32[192,2880]{1,0:T(8,128)}, u32[]{:S(2)}) copy-start(f32[192,2880]{1,0:T(8,128)} %mom_ref.1) | copy-start | bytes 6635524
  113.7 1.6 %copy-start.2 = (f32[192,2880]{1,0:T(8,128)S(1)}, f32[192,2880]{1,0:T(8,128)}, u32[]{:S(2)}) copy-start(f32[192,2880]{1,0:T(8,128)} %squ_ref.1) | copy-start | bytes 6635524
  115.3 1.3 %copy-start.3 = (bf16[4,2,4,48,384]{4,3,2,1,0:T(8,128)(2,1)S(1)}, bf16[4,2,4,48,384]{4,3,2,1,0:T(8,128)(2,1)}, u32[]{:S(2)}) copy-start(bf16[4,2,4,48,384]{4,3,2,1,0:T(8,128)(2,1)} %get-tuple-element.17.g_ref) | copy-start | bytes 3538948
  116.6 1.0 copy-start.4
  117.6 0.9 copy-start.5
  118.5 0.7 copy-start.9
  119.2 0.7 copy-start.10

commit v2 on v1

v2 whole, which is shorter than its diff:
```python
import math
from functools import partial
from types import SimpleNamespace

import jax
import jax.numpy as jnp
from jax import lax
from jax.experimental import pallas as pl
from jax.experimental.pallas import tpu as pltpu
from jax.sharding import PartitionSpec as P

HD = 64
HG = 768
MESH = pl.DeviceIdType.MESH
f32 = jnp.float32
bf16 = jnp.bfloat16

eps_norm = 1e-12
beta_one = 0.9
beta_two = 0.999
adam_eps = 1e-06
step_count = 100.0
decay_rate = 0.01
learn_rate = 0.04
matrix_rate = 1.0
NEG = -1e30


def nn(a, b):
    return jnp.dot(a, b, preferred_element_type=f32)


def nt(a, b, **kw):
    return lax.dot_general(a, b, (((1,), (1,)), ((), ())), preferred_element_type=f32, **kw)


def eye(n, dtype=bf16):
    rows = lax.broadcasted_iota(jnp.int32, (n, n), 0)
    cols = lax.broadcasted_iota(jnp.int32, (n, n), 1)
    return (rows == cols).astype(dtype)


def flip(a):
    return nt(eye(a.shape[1]), a)


def split_bf16(a):
    high = a.astype(bf16)
    return high, (a - high.astype(f32)).astype(bf16)


def lane_sums(a):
    return nt(jnp.ones((8, a.shape[1]), bf16), a)[0:1]


def lane_sums_f32(a):
    high, low = split_bf16(a)
    return lane_sums(high) + lane_sums(low)


def lamb_moments(gradient, first_moment, second_moment):
    first_new = beta_one * first_moment + (1.0 - beta_one) * gradient
    second_new = beta_two * second_moment + (1.0 - beta_two) * gradient * gradient
    update = (
        first_new
        / (1.0 - beta_one**step_count)
        / (jnp.sqrt(second_new / (1.0 - beta_two**step_count)) + adam_eps)
    )
    return first_new, second_new, update


def gelu_pair(pre):
    half = 0.5 * (1.0 + lax.erf(pre * (2.0**-0.5)))
    slope = half + pre * (jnp.exp(-0.5 * pre * pre) * ((2.0 * math.pi) ** -0.5))
    return pre * half, slope


class Sizes:
    def __init__(self, mesh_shape, tokens, row_count):
        self.nr = mesh_shape["rows"]
        self.nb = mesh_shape["blk"]
        self.nt = mesh_shape["tp"]
        self.g, self.t = tokens
        self.d = self.g * self.nt
        self.heads = self.g // HD
        self.row = row_count
        self.ch = 128
        self.nc = self.t // self.ch
        self.wc = self.heads * self.ch
        self.half = HG // 2
        self.keep = self.nb <= 4
        owners = self.nb
        while self.nb % owners or self.g % (16 * owners):
            owners -= 1
        self.owners = owners
        self.rq = self.g // owners
        o = 3 * self.g
        self.lo = (o + self.d + HG, o + self.d, o, 0)
        self.width = (HG, HG, self.d, o)
        self.cols = self.lo[0] + HG
        self.vmem = (48 if self.keep else 62) * 2**20


def scratch_of(s):
    V = pltpu.VMEM
    D = pltpu.SemaphoreType.DMA
    T, G, nb, ntp, nc, CH = s.t, s.g, s.nb, s.nt, s.nc, s.ch
    kept = nb if s.keep else 1
    shapes = dict(
        w=V((G, s.cols), f32),
        v=V((12, G), f32),
        ids=V((1, s.row), jnp.int32),
        cot=V((G, T), bf16),
        mom=V((G, s.cols), f32),
        squ=V((G, s.cols), f32),
        xt=V((nb, G, T), bf16),
        xtf=V((ntp, G, T), bf16),
        wot=V((ntp, 2, s.d // 2, G), bf16),
        vec=V((ntp, 16, G), f32),
        ctxg=V((nc, s.d, CH), bf16),
        st1=V((nc, ntp, 8, CH), f32),
        dmgg=V((nc, s.d, CH), bf16),
        st2=V((nc, ntp, 8, CH), f32),
        nrm=V((ntp, 16, 128), f32),
        dxr=V((nb, G, T), bf16),
        gcore=V((4, G, s.half), bf16),
        gz=V((4, nb, s.rq, s.half), bf16),
        gfin=V((4, 2, s.owners, s.rq, s.half), bf16),
        vgc=V((16, G), f32),
        vgz=V((nb, 16, G), f32),
        dxs=V((nb, G, T), bf16),
        gsrc=V((4, 2, G, s.half), bf16),
        ghalf=V((4, s.owners, s.rq, s.half), bf16),
        vgl=V((16, G), f32),
        vgs=V((16, G), f32),
        x=V((kept, T, G), bf16),
        keys_t=V((kept, G, T), bf16),
        vals=V((kept, T, G), bf16),
        wq=V((G, G), bf16),
        wq_t=V((G, G), bf16),
        wk=V((G, G), bf16),
        wk_t=V((G, G), bf16),
        wv=V((G, G), bf16),
        wv_t=V((G, G), bf16),
        wo=V((G, s.d), bf16),
        wof=V((s.d, s.d), bf16),
        w1=V((G, HG), bf16),
        w1_t=V((HG, G), bf16),
        w2=V((G, HG), bf16),
        w2_t=V((HG, G), bf16),
        qz=V((nc, G, s.wc), bf16),
        dcz=V((nc, G, s.wc), bf16),
        idk=V((kept, T, 128), f32),
        ebuf=V((kept, nc, T, s.wc), bf16),
        mrec=V((kept, nc, 1, s.wc), f32),
        mrun=V((nc, 1, s.wc), f32),
        lrun=V((nc, 1, s.wc), f32),
        acc=V((G, T), f32),
        ctxl=V((G, T), bf16),
        delta=V((nc, 1, s.wc), f32),
        lse=V((nc, 1, s.wc), f32),
        n1f=V((nc, s.d, CH), f32),
        inv1=V((nc, 1, CH), f32),
        datt=V((s.d, T), bf16),
        act=V((HG, T), bf16),
        slope=V((HG, T), f32),
        dpre=V((HG, T), bf16),
        midl=V((G, T), bf16),
        dffn=V((G, T), bf16),
        h2=V((G, T), f32),
        cn2=V((G, T), f32),
        dmid=V((G, T), f32),
        dmn1=V((G, T), f32),
        dqt=V((G, T), f32),
        dkb=V((kept, T, G), f32),
        dvb=V((kept, T, G), f32),
        gkv=V((2, G, G), f32),
        vb=V((1, G), f32),
        dxo=V((G, T), f32),
        x_s=D((nb,)), x_r=D((nb,)),
        xtf_s=D((ntp,)), xtf_r=D((ntp,)),
        wot_s=D((ntp,)), wot_r=D((ntp,)),
        woc_s=D((ntp,)), woc_r=D((ntp,)),
        vec_s=D((ntp,)), vec_r=D((ntp,)),
        ctx_s=D((nc, ntp)), ctx_r=D((nc, ntp)),
        st1_s=D((nc, ntp)), st1_r=D((nc, ntp)),
        dmg_s=D((nc, ntp)), dmg_r=D((nc, ntp)),
        st2_s=D((nc, ntp)), st2_r=D((nc, ntp)),
        nrm_s=D((ntp,)), nrm_r=D((ntp,)),
        dx_s=D((nb,)), dx_r=D((nb,)),
        gc_s=D((4,)), gc_r=D((4,)),
        gz_s=D((4, nb)), gz_r=D((4, nb)),
        ga_s=D((4, nb)), ga_r=D((4, nb)),
        gd_s=D((4,)), gd_r=D((4,)),
        vc_s=D((1,)), vc_r=D((1,)),
        vz_s=D((nb,)), vz_r=D((nb,)),
        loc=D((8,)),
        put=D((8,)),
    )
    return list(shapes.keys()), list(shapes.values())


def layer_kernel(s, names, x_hbm, cot_hbm, ids_hbm, w_hbm, v_hbm, mom_hbm, squ_hbm,
                 out_hbm, ig_hbm, g_hbm, vg_hbm, ratio_hbm, out_ref, ig_ref, vg_ref, ratio_ref, *scratch):
    r = SimpleNamespace(**dict(zip(names, scratch)))
    T, G, nb, ntp, nc, CH = s.t, s.g, s.nb, s.nt, s.nc, s.ch
    c, b, t = lax.axis_index("rows"), lax.axis_index("blk"), lax.axis_index("tp")
    core = (1 - c, b, t)
    tx, ty = t % 2, t // 2
    tp_peers = [ty * 2 + (1 - tx), (1 - ty) * 2 + tx, 3 - t]
    if nb == 4:
        z_peers = [b + 1 - 2 * (b % 2), (b + 2) % 4, 3 - b]
    else:
        z_peers = [(b + o) % nb for o in range(1, nb)]

    def tp_dev(k):
        return (c, b, k)

    def z_dev(k):
        return (c, k, t)

    sent = []
    pending = {}

    def copy(src, dst, ssem, rsem, dev):
        return pltpu.make_async_remote_copy(
            src_ref=src, dst_ref=dst, send_sem=ssem, recv_sem=rsem, device_id=dev, device_id_type=MESH
        )

    def push(key, src, dst, ssem, rsem, dev, here, here_sem):
        one = copy(src, dst, ssem, rsem, dev)
        one.start()
        sent.append(one)
        pending[key] = copy(here, here, ssem, here_sem, dev)

    def arrive(key):
        pending.pop(key).wait_recv()

    def tp_push(key, at, sems):
        ssem, rsem = sems
        for i, k in enumerate(tp_peers):
            push((key, i), at(t), at(t), ssem(k), rsem(t), tp_dev(k), at(k), rsem(k))

    def tp_arrive(key):
        for i in range(ntp - 1):
            arrive((key, i))

    def sems(leaving, landing, *lead):
        return lambda k: leaving.at[lead + (k,)], lambda k: landing.at[lead + (k,)]

    def group(k):
        return pl.ds(pl.multiple_of(k * G, G), G)

    def load(i, src, dst):
        one = pltpu.make_async_copy(src, dst, r.loc.at[i])
        one.start()
        return one

    stored = []

    def store(src, dst):
        one = pltpu.make_async_copy(src, dst, r.put.at[len(stored)])
        one.start()
        stored.append(one)

    barrier = pltpu.get_barrier_semaphore()
    pl.semaphore_signal(barrier, 1, device_id=core, device_id_type=MESH)
    for k in tp_peers:
        pl.semaphore_signal(barrier, 1, device_id=tp_dev(k), device_id_type=MESH)
    for k in z_peers:
        pl.semaphore_signal(barrier, 1, device_id=z_dev(k), device_id_type=MESH)
    load_x = load(0, x_hbm, r.xt.at[b])
    load_v = load(1, v_hbm, r.v)
    load_ids = load(2, ids_hbm, r.ids)
    load_w = load(3, w_hbm, r.w)
    load_cot = load(4, cot_hbm, r.cot)
    load_m = load(5, mom_hbm, r.mom)
    load_s = load(6, squ_hbm, r.squ)
    load_x.wait()
    load_v.wait()
    load_ids.wait()
    r.xtf[t] = r.xt[b]
    r.vec[t, 0:12, :] = r.v[...]
    r.vec[t, 12:16, :] = jnp.zeros((4, G), f32)
    load_w.wait()
    w_ref = r.w
    w_o = w_ref[:, s.lo[2]:s.lo[2] + s.d].astype(bf16)
    r.wo[...] = w_o
    w_ot = flip(w_o).astype(bf16)
    r.wot[t, 0] = w_ot[:s.d // 2]
    r.wot[t, 1] = w_ot[s.d // 2:]
    pl.semaphore_wait(barrier, 1 + (ntp - 1) + (nb - 1))

    for i, j in enumerate(z_peers):
        push(("x", i), r.xt.at[b], r.xt.at[b], r.x_s.at[j], r.x_r.at[b], z_dev(j), r.xt.at[j], r.x_r.at[j])
    tp_push("vec", lambda k: r.vec.at[k], sems(r.vec_s, r.vec_r))
    tp_push("xtf", lambda k: r.xtf.at[k], sems(r.xtf_s, r.xtf_r))
    tp_push("wot", lambda k: r.wot.at[k, c], sems(r.wot_s, r.wot_r))

    w_q = w_ref[:, 0:G].astype(bf16)
    w_k = w_ref[:, G:2 * G].astype(bf16)
    w_v = w_ref[:, 2 * G:3 * G].astype(bf16)
    r.wq[...] = w_q
    r.wq_t[...] = flip(w_q).astype(bf16)
    r.wk[...] = w_k
    r.wk_t[...] = flip(w_k).astype(bf16)
    r.wv[...] = w_v
    r.wv_t[...] = flip(w_v).astype(bf16)

    def columns_of(vec):
        return nt(eye(G, f32), vec, precision=lax.Precision.HIGHEST)

    v_cols = columns_of(r.vec[t])

    def v_col(k):
        return v_cols[:, k:k + 1]

    bias_v_row = r.v[1:2, :]
    bias_v_col = v_col(1)

    scaling = HD**-0.5
    q_t = (nn(r.wq_t[...], r.xt[b]) + v_col(0)).astype(bf16)
    q_t = q_t.astype(f32) * scaling
    head_of = lax.broadcasted_iota(jnp.int32, (G, CH), 0) // HD

    def by_head(a):
        return jnp.concatenate([jnp.where(head_of == h, a, 0.0).astype(bf16) for h in range(s.heads)], axis=1)

    def lanes(k):
        return slice(k * CH, (k + 1) * CH)

    def head_rows(h):
        return slice(h * HD, (h + 1) * HD)

    for k in range(nc):
        r.qz[k] = by_head(q_t[:, lanes(k)])

    def ids_of(j):
        return r.ids[:, pl.ds(pl.multiple_of(j * T, 128), T)].astype(f32)

    def id_columns(j):
        ids = ids_of(j)
        high = jnp.floor(ids * (1.0 / 128.0))
        low = ids - 128.0 * high
        high, low = (jnp.broadcast_to(a, (128, T)).astype(bf16) for a in (high, low))
        return 128.0 * nt(eye(T), high) + nt(eye(T), low)

    if s.keep:
        for k in range(nb):
            r.idk[k] = id_columns(k)
    id_q = ids_of(b)

    r.mrun[...] = jnp.full((nc, 1, s.wc), NEG, f32)
    r.lrun[...] = jnp.zeros((nc, 1, s.wc), f32)
    r.acc[...] = jnp.zeros((G, T), f32)

    def same_doc(j, k):
        ids = r.idk[j] if s.keep else id_columns(j)
        return jnp.concatenate([ids == id_q[:, lanes(k)]] * s.heads, axis=1)

    def forward_block(j, after=None):
        x_jt = r.xt[j]
        x_j = flip(x_jt).astype(bf16)
        keys = nn(x_j, r.wk[...]).astype(bf16)
        vals_t = (nn(r.wv_t[...], x_jt) + bias_v_col).astype(bf16)
        for k in range(nc):
            score = jnp.where(same_doc(j, k), nn(keys, r.qz[k]), NEG)
            old = r.mrun[k]
            top = jnp.maximum(old, jnp.max(score, axis=0, keepdims=True))
            fade = jnp.exp(old - top)
            e = jnp.exp(score - top)
            r.lrun[k] = r.lrun[k] * fade + jnp.sum(e, axis=0, keepdims=True)
            e = e.astype(bf16)
            if s.keep:
                r.ebuf[j, k] = e
                r.mrec[j, k] = top
            r.mrun[k] = top
            for h in range(s.heads):
                rows = head_rows(h)
                r.acc[rows, lanes(k)] = r.acc[rows, lanes(k)] * fade[:, lanes(h)] + nn(vals_t[rows, :], e[:, lanes(h)])
            if after is not None:
                after(k)
        if s.keep:
            r.x[j] = x_j
            r.keys_t[j] = nn(r.wk_t[...], x_jt).astype(bf16)
            r.vals[j] = (nn(x_j, r.wv[...]) + bias_v_row).astype(bf16)

    forward_block(b)

    w_1 = w_ref[:, s.lo[1]:s.lo[1] + HG].astype(bf16)
    w_2 = w_ref[:, s.lo[0]:s.lo[0] + HG].astype(bf16)
    r.w1[...] = w_1
    r.w1_t[...] = flip(w_1).astype(bf16)
    r.w2[...] = w_2
    r.w2_t[...] = flip(w_2).astype(bf16)
    load_cot.wait()
    load_m.wait()
    load_s.wait()

    def context_ready(k):
        r.lse[k] = r.mrun[k] + jnp.log(r.lrun[k])
        inverse = 1.0 / r.lrun[k]
        parts = [r.acc[head_rows(h), lanes(k)] * inverse[:, lanes(h)] for h in range(s.heads)]
        context = jnp.concatenate(parts, axis=0)
        r.acc[:, lanes(k)] = context
        context = context.astype(bf16)
        r.ctxl[:, lanes(k)] = context
        r.ctxg[k, group(t), :] = context
        tp_push(("ctx", k), lambda d: r.ctxg.at[k, group(d), :], sems(r.ctx_s, r.ctx_r, k))

    if s.keep:
        for i, j in enumerate(z_peers):
            arrive(("x", i))
            forward_block(j, context_ready if i == nb - 2 else None)
    else:
        def forward_remote(o, _):
            j = (b + o) % nb
            copy(r.xt.at[j], r.xt.at[j], r.x_s.at[j], r.x_r.at[j], z_dev(j)).wait_recv()
            forward_block(j)
            return 0

        lax.fori_loop(1, nb, forward_remote, 0)
        for i in range(nb - 1):
            pending.pop(("x", i))
        for k in range(nc):
            context_ready(k)

    tp_arrive("wot")
    for i, k in enumerate(tp_peers):
        push(("woc", i), r.wot.at[k, c], r.wot.at[k, c], r.woc_s.at[k], r.woc_r.at[k], core, r.wot.at[k, 1 - c], r.woc_r.at[k])
    tp_arrive("vec")
    tp_arrive("xtf")
    out_bias = [columns_of(r.vec[k])[:, 2:3] for k in range(ntp)]
    tp_arrive("woc")
    for k in range(ntp):
        for h in range(2):
            r.wof[h * (s.d // 2):(h + 1) * (s.d // 2), k * G:(k + 1) * G] = r.wot[k, h]

    gain1 = v_col(3)
    bias_rows = HG // G
    hid_bias = jnp.concatenate([v_col(5 + k) for k in range(bias_rows)], axis=0)
    gain2 = v_col(6 + bias_rows)
    shift2 = v_col(7 + bias_rows)

    def forward_chunk(k):
        tp_arrive(("ctx", k))
        att = nn(r.wof[...], r.ctxg[k])
        hidden = [
            r.xtf[d][:, lanes(k)].astype(f32) + att[d * G:(d + 1) * G] + out_bias[d] for d in range(ntp)
        ]
        mean = sum(jnp.sum(a, axis=0, keepdims=True) for a in hidden) / s.d
        hidden = [a - mean for a in hidden]
        var = sum(jnp.sum(a * a, axis=0, keepdims=True) for a in hidden) / s.d
        inv = lax.rsqrt(var + eps_norm)
        r.inv1[k] = inv
        for d in range(ntp):
            r.n1f[k, d * G:(d + 1) * G, :] = hidden[d] * inv
        mid = r.n1f[k, group(t), :] * gain1 + v_col(4)
        mid_low = mid.astype(bf16)
        r.midl[:, lanes(k)] = mid_low
        act, slope = gelu_pair(nn(r.w1_t[...], mid_low) + hid_bias)
        act = act.astype(bf16)
        r.act[:, lanes(k)] = act
        r.slope[:, lanes(k)] = slope
        h2 = mid + nn(r.w2[...], act) + v_col(5 + bias_rows)
        r.h2[:, lanes(k)] = h2
        scaled = r.cot[:, lanes(k)].astype(f32) * gain2
        sum1 = jnp.sum(h2, axis=0, keepdims=True)
        h2c = h2 - sum1 / G
        sum2 = jnp.sum(h2c * h2c, axis=0, keepdims=True)
        sum3 = jnp.sum(scaled, axis=0, keepdims=True)
        sum4 = jnp.sum(scaled * h2c, axis=0, keepdims=True)
        r.st1[k, t] = jnp.concatenate([sum1, sum2, sum3, sum4, jnp.zeros((4, CH), f32)], axis=0)
        tp_push(("st1", k), lambda d: r.st1.at[k, d], sems(r.st1_s, r.st1_r, k))

    def backward_chunk(k):
        tp_arrive(("st1", k))
        stats = [r.st1[k, d] for d in range(ntp)]
        mean = sum(a[0:1] for a in stats) / s.d
        offs = [a[0:1] / G - mean for a in stats]
        var = sum(a[1:2] + G * o * o for a, o in zip(stats, offs)) / s.d
        inv = lax.rsqrt(var + eps_norm)
        first = sum(a[2:3] for a in stats) / s.d
        second = sum(a[3:4] + a[2:3] * o for a, o in zip(stats, offs)) * inv / s.d
        n2 = (r.h2[:, lanes(k)] - mean) * inv
        out_ref[:, lanes(k)] = (n2 * gain2 + shift2).astype(bf16)
        cot = r.cot[:, lanes(k)].astype(f32)
        r.cn2[:, lanes(k)] = cot * n2
        d2 = inv * (cot * gain2 - first - n2 * second)
        dffn = d2.astype(bf16)
        r.dffn[:, lanes(k)] = dffn
        dpre = (nn(r.w2_t[...], dffn) * r.slope[:, lanes(k)]).astype(bf16)
        r.dpre[:, lanes(k)] = dpre
        dmid = d2 + nn(r.w1[...], dpre)
        r.dmid[:, lanes(k)] = dmid
        n1 = r.n1f[k, group(t), :]
        r.dmn1[:, lanes(k)] = dmid * n1
        dmg = dmid * gain1
        part1 = jnp.sum(dmg, axis=0, keepdims=True)
        part2 = jnp.sum(dmg * n1, axis=0, keepdims=True)
        r.st2[k, t] = jnp.concatenate([part1, part2, jnp.zeros((6, CH), f32)], axis=0)
        r.dmgg[k, group(t), :] = dmg.astype(bf16)
        tp_push(("st2", k), lambda d: r.st2.at[k, d], sems(r.st2_s, r.st2_r, k))
        tp_push(("dmg", k), lambda d: r.dmgg.at[k, group(d), :], sems(r.dmg_s, r.dmg_r, k))

    for k in range(nc):
        forward_chunk(k)
    for k in range(nc):
        backward_chunk(k)
    store(out_ref, out_hbm)

    def sum_start(m):
        push(("gc", m), r.gsrc.at[m, 1 - c], r.gcore.at[m], r.gc_s.at[m], r.gc_r.at[m], core, r.gcore.at[m], r.gc_r.at[m])

    def when_owner(j, body):
        if s.owners < nb:
            pl.when(j < s.owners)(body)
        else:
            body()

    def to_owner(m, j):
        return copy(r.ghalf.at[m, j], r.gz.at[m, b], r.gz_s.at[m, j], r.gz_r.at[m, b], z_dev(j))

    def to_all(m, j):
        mine = r.gfin.at[m, c, b]
        return copy(mine, mine, r.ga_s.at[m, j], r.ga_r.at[m, b], z_dev(j))

    def sum_spread(m):
        arrive(("gc", m))
        both = (r.gsrc[m, c].astype(f32) + r.gcore[m].astype(f32)).astype(bf16)
        for k in range(s.owners):
            r.ghalf[m, k] = both[k * s.rq:(k + 1) * s.rq]
        for j in z_peers:
            when_owner(j, lambda: to_owner(m, j).start())

    def sum_own(m):
        def body():
            for j in z_peers:
                copy(r.gz.at[m, j], r.gz.at[m, j], r.gz_s.at[m, 0], r.gz_r.at[m, j], z_dev(j)).wait_recv()
            r.gz[m, b] = r.ghalf[m, b]
            total = r.gz[m, 0].astype(f32)
            for j in range(1, nb):
                total = total + r.gz[m, j].astype(f32)
            r.gfin[m, c, b] = total.astype(bf16)
            for j in z_peers:
                to_all(m, j).start()

        when_owner(b, body)

    def sum_share(m):
        for j in z_peers:
            slot = r.gfin.at[m, c, j]
            when_owner(j, lambda: copy(slot, slot, r.ga_s.at[m, 0], r.ga_r.at[m, j], z_dev(j)).wait_recv())
        push(("gd", m), r.gfin.at[m, c], r.gfin.at[m, c], r.gd_s.at[m], r.gd_r.at[m], core, r.gfin.at[m, 1 - c], r.gd_r.at[m])

    def sum_done(m):
        arrive(("gd", m))
        store(r.gfin.at[m], g_hbm.at[m])

    def sum_sends_done(m):
        for j in z_peers:
            when_owner(j, lambda: to_owner(m, j).wait_send())

        def body():
            for j in z_peers:
                to_all(m, j).wait_send()

        when_owner(b, body)

    def keep_grad(m, grad):
        r.gsrc[m, 0] = grad[:, 0:s.half].astype(bf16)
        r.gsrc[m, 1] = grad[:, s.half:].astype(bf16)

    keep_grad(0, nt(r.dffn[...], r.act[...]))
    sum_start(0)
    keep_grad(1, nt(r.midl[...], r.dpre[...]))
    sum_start(1)
    vgl = r.vgl
    vgl[12:16, :] = jnp.zeros((4, G), f32)
    vgl[3:4, :] = lane_sums_f32(r.dmn1[...])
    vgl[4:5, :] = lane_sums_f32(r.dmid[...])
    hid_sum = lane_sums(r.dpre[...])
    for k in range(bias_rows):
        vgl[5 + k:6 + k, :] = hid_sum[:, k * G:(k + 1) * G]
    vgl[5 + bias_rows:6 + bias_rows, :] = lane_sums(r.dffn[...])
    vgl[6 + bias_rows:7 + bias_rows, :] = lane_sums_f32(r.cn2[...])
    vgl[7 + bias_rows:8 + bias_rows, :] = lane_sums(r.cot[...])

    def context_chunk(k):
        tp_arrive(("st2", k))
        stats = [r.st2[k, d] for d in range(ntp)]
        first = sum(a[0:1] for a in stats) / s.d
        second = sum(a[1:2] for a in stats) / s.d
        inv = r.inv1[k]
        own = inv * (r.dmid[:, lanes(k)] * gain1 - first - r.n1f[k, group(t), :] * second)
        r.dxo[:, lanes(k)] = own
        tp_arrive(("dmg", k))
        for d in range(ntp):
            rows = slice(d * G, (d + 1) * G)
            part = inv * (r.dmgg[k, rows, :].astype(f32) - first - r.n1f[k, rows, :] * second)
            r.datt[rows, lanes(k)] = part.astype(bf16)
        dctx = nn(r.wo[...], r.datt[:, lanes(k)]).astype(bf16).astype(f32)
        r.dcz[k] = by_head(dctx)
        parts = [
            jnp.sum(dctx[head_rows(h)] * r.acc[head_rows(h), lanes(k)], axis=0, keepdims=True)
            for h in range(s.heads)
        ]
        r.delta[k] = jnp.concatenate(parts, axis=1)

    r.dqt[...] = jnp.zeros((G, T), f32)
    r.gkv[...] = jnp.zeros((2, G, G), f32)
    r.vb[...] = jnp.zeros((1, G), f32)

    def pair_terms(j, chunks):
        if s.keep:
            keys_t, vals = r.keys_t[j], r.vals[j]
        else:
            x_jt = r.xt[j]
            x_j = flip(x_jt).astype(bf16)
            keys_t = nn(r.wk_t[...], x_jt).astype(bf16)
            vals = (nn(x_j, r.wv[...]) + bias_v_row).astype(bf16)
            keys = nn(x_j, r.wk[...]).astype(bf16)
        dk = dv = None
        for k in chunks:
            if s.keep:
                p = r.ebuf[j, k].astype(f32) * jnp.exp(r.mrec[j, k] - r.lse[k])
            else:
                p = jnp.exp(jnp.where(same_doc(j, k), nn(keys, r.qz[k]), NEG) - r.lse[k])
            ds = (p * (nn(vals, r.dcz[k]) - r.delta[k])).astype(bf16)
            p = p.astype(bf16)
            for h in range(s.heads):
                r.dqt[head_rows(h), lanes(k)] += nn(keys_t[head_rows(h), :], ds[:, lanes(h)])
            dk_k, dv_k = nt(ds, r.qz[k]), nt(p, r.dcz[k])
            dk, dv = (dk_k, dv_k) if dk is None else (dk + dk_k, dv + dv_k)
        return dk, dv

    def finish_block(j, dk, dv):
        dk, dv = dk.astype(bf16), dv.astype(bf16)
        x_jt = r.xt[j]
        r.gkv[0] += nn(x_jt, dk)
        r.gkv[1] += nn(x_jt, dv)
        r.vb[...] += jnp.sum(dv.astype(f32), axis=0, keepdims=True)
        return nt(r.wk[...], dk) + nt(r.wv[...], dv)

    def dx_send(j):
        return copy(r.dxs.at[j], r.dxr.at[b], r.dx_s.at[j], r.dx_r.at[b], z_dev(j))

    if s.keep:
        context_chunk(0)
        sum_spread(0)
        sum_spread(1)
        for j in z_peers + [b]:
            r.dkb[j], r.dvb[j] = pair_terms(j, [0])
        for k in range(1, nc):
            context_chunk(k)
        keep_grad(2, nt(r.ctxl[...], r.datt[...]))
        sum_start(2)
        vgl[2:3, :] = lane_sums(r.dxo[...].astype(bf16))
        sum_own(0)
        sum_own(1)
        for i, j in enumerate(z_peers):
            dk, dv = pair_terms(j, range(1, nc))
            r.dxs[j] = finish_block(j, dk + r.dkb[j], dv + r.dvb[j]).astype(bf16)
            dx_send(j).start()
            if i == 0:
                sum_spread(2)
            if i == nb - 2:
                sum_share(0)
                sum_share(1)
        dk, dv = pair_terms(b, range(1, nc))
        r.dxo[...] += finish_block(b, dk + r.dkb[b], dv + r.dvb[b])
    else:
        for k in range(nc):
            context_chunk(k)
        keep_grad(2, nt(r.ctxl[...], r.datt[...]))
        sum_start(2)
        vgl[2:3, :] = lane_sums(r.dxo[...].astype(bf16))

        def backward_remote(o, _):
            j = (b + o) % nb
            r.dxs[j] = finish_block(j, *pair_terms(j, range(nc))).astype(bf16)
            dx_send(j).start()
            return 0

        lax.fori_loop(1, nb, backward_remote, 0)
        r.dxo[...] += finish_block(b, *pair_terms(b, range(nc)))
        for m in (0, 1, 2):
            sum_spread(m)
        sum_own(0)
        sum_own(1)
        sum_share(0)
        sum_share(1)
    dq_t = (r.dqt[...] * scaling).astype(bf16)
    r.gsrc[3, 0, :, 0:G] = nt(r.xt[b], dq_t).astype(bf16)
    r.gsrc[3, 0, :, G:2 * G] = r.gkv[0].astype(bf16)
    r.gsrc[3, 1, :, 0:G] = r.gkv[1].astype(bf16)
    r.gsrc[3, 1, :, G:2 * G] = jnp.zeros((G, G), bf16)
    sum_start(3)
    vgl[0:1, :] = lane_sums(dq_t)
    vgl[1:2, :] = r.vb[...]
    push(("vc",), vgl, r.vgc, r.vc_s.at[0], r.vc_r.at[0], core, r.vgc, r.vc_r.at[0])
    sum_spread(3)
    arrive(("vc",))
    r.vgs[...] = vgl[...] + r.vgc[...]
    r.vgz[b] = r.vgs[...]
    for i, j in enumerate(z_peers):
        push(("vz", i), r.vgs, r.vgz.at[b], r.vz_s.at[j], r.vz_r.at[b], z_dev(j), r.vgz.at[j], r.vz_r.at[j])
    r.dxo[...] += nn(r.wq[...], dq_t)
    sum_own(2)

    def norms_of(m):
        rows = []
        for h in range(2):
            lo = s.lo[m] + h * s.half
            wide = min(s.half, s.lo[m] + s.width[m] - lo)
            grad = jnp.concatenate([r.gfin[m, h, k] for k in range(s.owners)], axis=0)[:, :wide]
            w = w_ref[:, lo:lo + wide]
            _, _, u = lamb_moments(grad.astype(f32), r.mom[:, lo:lo + wide], r.squ[:, lo:lo + wide])
            u = u + decay_rate * w
            rows.append((jnp.sum(w * w, axis=0, keepdims=True), jnp.sum(u * u, axis=0, keepdims=True)))
        return rows

    def total(a):
        return jnp.broadcast_to(jnp.sum(a, axis=1, keepdims=True), (1, 128))

    sums = {}
    for m in (0, 1):
        sum_done(m)
        sums[m] = norms_of(m)
    sum_own(3)
    sum_share(2)
    for i, j in enumerate(z_peers):
        copy(r.dxr.at[j], r.dxr.at[j], r.dx_s.at[j], r.dx_r.at[j], z_dev(j)).wait_recv()
        r.dxo[...] += r.dxr[j].astype(f32)
    ig_ref[...] = r.dxo[...]
    store(ig_ref, ig_hbm)
    sum_done(2)
    sums[2] = norms_of(2)
    sum_share(3)
    for i in range(nb - 1):
        arrive(("vz", i))
    vg = r.vgz[0]
    for j in range(1, nb):
        vg = vg + r.vgz[j]
    vg_ref[...] = vg[0:12]
    store(vg_ref, vg_hbm)
    sum_done(3)
    sums[3] = norms_of(3)
    packed = []
    for which in range(2):
        lead = sums[3][0][which]
        packed += [total(lead[:, 0:G]), total(lead[:, G:2 * G]), total(sums[3][1][which])]
        packed += [total(sums[m][0][which] + sums[m][1][which]) for m in (2, 1, 0)]
        packed += [jnp.zeros((2, 128), f32)]
    r.nrm[t] = jnp.concatenate(packed, axis=0)
    tp_push("nrm", lambda k: r.nrm.at[k], sems(r.nrm_s, r.nrm_r))
    tp_arrive("nrm")
    norms = r.nrm[0]
    for k in range(1, ntp):
        norms = norms + r.nrm[k]
    ratio_ref[...] = jnp.sqrt(norms[0:8] / (norms[8:16] + 1e-12))
    store(ratio_ref, ratio_hbm)

    for one in sent:
        one.wait_send()
    for m in range(4):
        sum_sends_done(m)
    for j in z_peers:
        dx_send(j).wait_send()
    for one in stored:
        one.wait()


def finish_kernel(s, out_in, ig_in, w_ref, mom_ref, squ_ref, g_ref, ratio_ref, v_ref, vg_ref, mv_ref, sv_ref,
                  out_ref, ig_ref, gm_ref, gv_ref, nm_ref, ns_ref, nmv_ref, nsv_ref, nw_ref, nv_ref, grad):
    out_ref[...] = out_in[...]
    ig_ref[...] = ig_in[...]
    for m in range(4):
        for h in range(2):
            lo = s.lo[m] + h * s.half
            wide = min(s.half, s.lo[m] + s.width[m] - lo)
            grad[:, lo:lo + wide] = g_ref[m, h, 0, :, 0:wide].astype(f32)
    cols = s.cols
    g = grad[...]
    gm_ref[...] = g
    new_m, new_s, u = lamb_moments(g, mom_ref[...], squ_ref[...])
    nm_ref[...] = new_m
    ns_ref[...] = new_s
    w = w_ref[...]
    u = u + decay_rate * w
    col = lax.broadcasted_iota(jnp.int32, (1, cols), 1)
    ratio = jnp.broadcast_to(ratio_ref[5:6, 0:1], (1, cols))
    for k, edge in ((4, s.lo[0]), (3, s.lo[1]), (2, s.lo[2]), (1, 2 * s.g), (0, s.g)):
        ratio = jnp.where(col < edge, ratio_ref[k:k + 1, 0:1], ratio)
    nw_ref[...] = w - matrix_rate * ratio * u

    @pl.when(pl.program_id(0) == 0)
    def _():
        vg = vg_ref[...]
        gv_ref[...] = vg
        new_mv, new_sv, uv = lamb_moments(vg, mv_ref[...], sv_ref[...])
        nmv_ref[...] = new_mv
        nsv_ref[...] = new_sv
        nv_ref[...] = v_ref[...] - learn_rate * uv


def local(mesh_shape, tokens, cotangent, segment_ids, matrices, vectors, moment_mat, square_mat, moment_vec, square_vec):
    tokens, cotangent = tokens.T, cotangent.T
    s = Sizes(mesh_shape, tokens.shape, segment_ids.shape[1])
    names, scratch = scratch_of(s)
    hbm = pl.BlockSpec(memory_space=pltpu.HBM)
    S = jax.ShapeDtypeStruct
    small = [
        pltpu.VMEM(tokens.shape, bf16), pltpu.VMEM(tokens.shape, f32),
        pltpu.VMEM(vectors.shape, f32), pltpu.VMEM((8, 128), f32),
    ]
    given = (tokens, cotangent, segment_ids, matrices, vectors, moment_mat, square_mat)
    output, input_grad, grads, vector_grad, ratio = pl.pallas_call(
        partial(layer_kernel, s, names),
        out_shape=(
            S(tokens.shape, bf16),
            S(tokens.shape, f32),
            S((4, 2, s.owners, s.rq, s.half), bf16),
            S(vectors.shape, f32),
            S((8, 128), f32),
        ),
        in_specs=[hbm] * 7,
        out_specs=(hbm,) * 5,
        scratch_shapes=small + scratch,
        compiler_params=pltpu.CompilerParams(
            collective_id=0, has_side_effects=True, vmem_limit_bytes=s.vmem
        ),
        name="layer",
    )(*(pltpu.with_memory_space_constraint(a, pltpu.HBM) for a in given))

    steps = s.owners

    def rows(a, n):
        return pl.BlockSpec((n, a.shape[1]), lambda i: (i, 0))

    def whole(a):
        return pl.BlockSpec(a.shape, lambda i: (0, 0))

    mat = rows(matrices, s.rq)
    vec = whole(vectors)
    results = pl.pallas_call(
        partial(finish_kernel, s),
        grid=(steps,),
        out_shape=(
            S(tokens.shape, bf16),
            S(tokens.shape, f32),
            S(matrices.shape, f32),
            S(vectors.shape, f32),
            S(matrices.shape, f32),
            S(matrices.shape, f32),
            S(vectors.shape, f32),
            S(vectors.shape, f32),
            S(matrices.shape, f32),
            S(vectors.shape, f32),
        ),
        in_specs=[
            rows(tokens, s.rq), rows(tokens, s.rq), mat, mat, mat,
            pl.BlockSpec((4, 2, 1, s.rq, s.half), lambda i: (0, 0, i, 0, 0)),
            pl.BlockSpec((8, 128), lambda i: (0, 0)), vec, vec, vec, vec,
        ],
        out_specs=(rows(tokens, s.rq), rows(tokens, s.rq), mat, vec, mat, mat, vec, vec, mat, vec),
        scratch_shapes=[pltpu.VMEM((s.rq, s.lo[0] + HG), f32)],
        compiler_params=pltpu.CompilerParams(vmem_limit_bytes=40 * 2**20),
        name="finish",
    )(output, input_grad, matrices, moment_mat, square_mat, grads, ratio, vectors, vector_grad, moment_vec, square_vec)
    return (results[0].T, results[1].T) + tuple(results[2:])


def solution(mesh):
    return jax.shard_map(
        partial(local, dict(mesh.shape)),
        mesh=mesh,
        in_specs=(
            P(("rows", "blk"), "tp"),
            P(("rows", "blk"), "tp"),
            P("rows", None),
            P("tp", None),
            P(None, "tp"),
            P("tp", None),
            P("tp", None),
            P(None, "tp"),
            P(None, "tp"),
        ),
        out_specs=(
            P(("rows", "blk"), "tp"),
            P(("rows", "blk"), "tp"),
            P("tp", None),
            P(None, "tp"),
            P("tp", None),
            P("tp", None),
            P(None, "tp"),
            P(None, "tp"),
            P("tp", None),
            P(None, "tp"),
        ),
        check_vma=False,
    )
```

time: 127 us -> 92.7 us (0.73)
  Pallas kernels: 113 us -> 91.7 us
  local copies, waits for them, and re-layouts: 13 us -> 0.03 us
    pallas_call x1, Pallas kernels: 108 us -> 86.7 us  [local(): pl.pallas_call(partial(layer_kernel, s, names), out_shape=(S(tokens.shape...]
    unnamed x24 -> x12, local copies, waits for them, and re-layouts: 11.3 us -> 0.03 us
    pallas_call x2 -> x0, local copies, waits for them, and re-layouts: 1.65 us -> none  [local(): pl.pallas_call(partial(finish_kernel, s), grid=(steps,), out_shape=(S(tok...]
where the time goes in v2:
time: 92.7 us; the launch traced here: 92.6 us
  Pallas kernels  91.7 us (99%)
    pallas_call x1, Pallas kernels, local(): pl.pallas_call(partial(layer_kernel, s, names), out_shape=(S(tokens.shape...  86.7 us
    pallas_call x1, Pallas kernels, local(): pl.pallas_call(partial(finish_kernel, s), grid=(steps,), out_shape=(S(tok...  4.97 us

profile of v2, /device:TPU:0, one launch (start us, length us, event | category | flops | bytes accessed | tf_op | source)
XLA Modules:
  0.0 92.6 jit_solution(15111695938667340038)
XLA Ops:
  0.6 0.0 copy-start
  0.7 0.0 copy-start.1
  0.7 0.0 copy-start.2
  0.7 0.0 copy-start.3
  0.7 0.0 copy-start.4
  0.7 0.0 copy-start.5
  0.7 86.7 %layer.1 = (bf16[192,384]{1,0:T(8,128)(2,1)S(1)}, f32[192,384]{1,0:T(8,128)S(1)}, bf16[4,2,4,48,384]{4,3,2,1,0:T(8,128)(2,1)S(1)}, f32[12,192]{1,0:T(8,128)S(1)}, f32[8,128]{1,0:T(8,128)S(1)}) custom-call(bf16[192,384]{1,0:T(8,128)(2,1)} %bitcast.4, bf16[192,384]{1,0:T(8,128)(2,1)} %bitcast.5, s32[1,1536]{1,0:T(1,128)} %ids_hbm.1, f32[192,2880]{1,0:T(8,128)} %w_ref.1, ...), custom_call_target="tpu_custom_call" | custom-call | tf_op jit(solution)/shard_map/layer/pallas_call | solution.py:818
  87.4 0.0 copy-done
  87.4 0.0 copy-done.1
  87.4 0.0 copy-done.2
  87.4 0.0 copy-done.3
  87.4 0.0 copy-done.4
  87.4 0.0 copy-done.5
  87.5 5.0 %finish.1 = (bf16[192,384]{1,0:T(8,128)(2,1)}, f32[192,384]{1,0:T(8,128)}, f32[192,2880]{1,0:T(8,128)}, f32[12,192]{1,0:T(8,128)}, f32[192,2880]{1,0:T(8,128)}, ...) custom-call(bf16[192,384]{1,0:T(8,128)(2,1)S(1)} %get-tuple-element., ...), custom_call_target="tpu_custom_call" | custom-call | tf_op jit(solution)/shard_map/finish/pallas_call | solution.py:846
Async XLA Ops:
  0.6 86.8 %copy-start = (f32[192,2880]{1,0:T(8,128)S(1)}, f32[192,2880]{1,0:T(8,128)}, u32[]{:S(2)}) copy-start(f32[192,2880]{1,0:T(8,128)} %w_ref.1) | copy-start | bytes 6635524
  0.7 86.8 %copy-start.1 = (f32[192,2880]{1,0:T(8,128)S(1)}, f32[192,2880]{1,0:T(8,128)}, u32[]{:S(2)}) copy-start(f32[192,2880]{1,0:T(8,128)} %mom_ref.1) | copy-start | bytes 6635524
  0.7 86.8 %copy-start.2 = (f32[192,2880]{1,0:T(8,128)S(1)}, f32[192,2880]{1,0:T(8,128)}, u32[]{:S(2)}) copy-start(f32[192,2880]{1,0:T(8,128)} %squ_ref.1) | copy-start | bytes 6635524
  0.7 86.8 %copy-start.3 = (f32[12,192]{1,0:T(8,128)S(1)}, f32[12,192]{1,0:T(8,128)}, u32[]{:S(2)}) copy-start(f32[12,192]{1,0:T(8,128)} %v_ref.1) | copy-start | bytes 27652
  0.7 86.8 %copy-start.4 = (f32[12,192]{1,0:T(8,128)S(1)}, f32[12,192]{1,0:T(8,128)}, u32[]{:S(2)}) copy-start(f32[12,192]{1,0:T(8,128)} %mv_ref.1) | copy-start | bytes 27652
  0.7 86.8 %copy-start.5 = (f32[12,192]{1,0:T(8,128)S(1)}, f32[12,192]{1,0:T(8,128)}, u32[]{:S(2)}) copy-start(f32[12,192]{1,0:T(8,128)} %sv_ref.1) | copy-start | bytes 27652

commit v3 on v2

--- a/solution.py
+++ b/solution.py
@@ -89,11 +89,16 @@
         self.wc = self.heads * self.ch
         self.half = HG // 2
         self.keep = self.nb <= 4
+        self.line = self.nb == 4
         owners = self.nb
         while self.nb % owners or self.g % (16 * owners):
             owners -= 1
         self.owners = owners
         self.rq = self.g // owners
+        tiles = 3 * self.g * self.g // (16 * 128)
+        self.pr = -(-tiles // (self.nr * owners)) * 16
+        self.ph = self.pr * owners
+        self.pack = self.ph * self.nr
         o = 3 * self.g
         self.lo = (o + self.d + HG, o + self.d, o, 0)
         self.width = (HG, HG, self.d, o)
@@ -115,22 +120,38 @@
         squ=V((G, s.cols), f32),
         xt=V((nb, G, T), bf16),
         xtf=V((ntp, G, T), bf16),
-        wot=V((ntp, 2, s.d // 2, G), bf16),
+        wot=V((ntp, 2, G // 2, s.d), bf16),
         vec=V((ntp, 16, G), f32),
         ctxg=V((nc, s.d, CH), bf16),
         st1=V((nc, ntp, 8, CH), f32),
         dmgg=V((nc, s.d, CH), bf16),
         st2=V((nc, ntp, 8, CH), f32),
-        nrm=V((ntp, 16, 128), f32),
+        nrm=V((ntp, 8, 128), f32),
         dxr=V((nb, G, T), bf16),
-        gcore=V((4, G, s.half), bf16),
-        gz=V((4, nb, s.rq, s.half), bf16),
-        gfin=V((4, 2, s.owners, s.rq, s.half), bf16),
+        dxa=V((nb if s.line else 1, G, T), bf16),
+        gcore=V((3, G, s.half), bf16),
+        gend=V((3, G, s.half) if s.line else (1, 16, 128), bf16),
+        gcross=V((3, G, s.half) if s.line else (1, 16, 128), bf16),
+        gz=V((1, 1, 16, 128) if s.line else (3, nb, s.rq, s.half), bf16),
+        gfin=V((3, 2, G, s.half), bf16),
+        qcore=V((s.ph, 128), bf16),
+        qz_in=V((nb, s.pr, 128), bf16),
+        qfin=V((s.pack, 128), bf16),
+        nq=V((s.nr, nb, 8, 128), f32),
+        nqt=V((ntp, 8, 128), f32),
+        upd=V((8, 128), f32),
         vgc=V((16, G), f32),
         vgz=V((nb, 16, G), f32),
         dxs=V((nb, G, T), bf16),
-        gsrc=V((4, 2, G, s.half), bf16),
-        ghalf=V((4, s.owners, s.rq, s.half), bf16),
+        gsrc=V((3, 2, G, s.half), bf16),
+        ghalf=V((3, G, s.half), bf16),
+        gmid=V((3, G, s.half) if s.line else (1, 16, 128), bf16),
+        qsrc=V((s.pack, 128), bf16),
+        qhalf=V((s.ph, 128), bf16),
+        gq=V((2, G, s.half), bf16),
+        pw=V((s.pack, 128), f32),
+        pm=V((s.pack, 128), f32),
+        ps=V((s.pack, 128), f32),
         vgl=V((16, G), f32),
         vgs=V((16, G), f32),
         x=V((kept, T, G), bf16),
@@ -142,7 +163,6 @@
         wk_t=V((G, G), bf16),
         wv=V((G, G), bf16),
         wv_t=V((G, G), bf16),
-        wo=V((G, s.d), bf16),
         wof=V((s.d, s.d), bf16),
         w1=V((G, HG), bf16),
         w1_t=V((HG, G), bf16),
@@ -177,7 +197,7 @@
         gkv=V((2, G, G), f32),
         vb=V((1, G), f32),
         dxo=V((G, T), f32),
-        x_s=D((nb,)), x_r=D((nb,)),
+        x_s=D((nb,)), x_r=D((nb,)), xf_s=D((1,)),
         xtf_s=D((ntp,)), xtf_r=D((ntp,)),
         wot_s=D((ntp,)), wot_r=D((ntp,)),
         woc_s=D((ntp,)), woc_r=D((ntp,)),
@@ -188,10 +208,19 @@
         st2_s=D((nc, ntp)), st2_r=D((nc, ntp)),
         nrm_s=D((ntp,)), nrm_r=D((ntp,)),
         dx_s=D((nb,)), dx_r=D((nb,)),
-        gc_s=D((4,)), gc_r=D((4,)),
-        gz_s=D((4, nb)), gz_r=D((4, nb)),
-        ga_s=D((4, nb)), ga_r=D((4, nb)),
-        gd_s=D((4,)), gd_r=D((4,)),
+        da_s=D((nb,)), da_r=D((nb,)),
+        gc_s=D((3,)), gc_r=D((3,)),
+        ge_s=D((3,)), ge_r=D((3,)),
+        gx_s=D((3,)), gx_r=D((3,)),
+        gz_s=D((3, nb)), gz_r=D((3, nb)),
+        ga_s=D((3, nb)), ga_r=D((3, nb)),
+        gd_s=D((3,)), gd_r=D((3,)),
+        qc_s=D((1,)), qc_r=D((1,)),
+        qz_s=D((nb,)), qz_r=D((nb,)),
+        qa_s=D((nb,)), qa_r=D((nb,)),
+        qd_s=D((1,)), qd_r=D((1,)),
+        nq_s=D((s.nr, nb)), nq_r=D((s.nr, nb)),
+        nqt_s=D((ntp,)), nqt_r=D((ntp,)),
         vc_s=D((1,)), vc_r=D((1,)),
         vz_s=D((nb,)), vz_r=D((nb,)),
         loc=D((8,)),
@@ -236,6 +265,13 @@
     def arrive(key):
         pending.pop(key).wait_recv()
 
+    sent_if = []
+
+    def push_if(who, src, dst, ssem, rsem, dev):
+        one = copy(src, dst, ssem, rsem, dev)
+        pl.when(who)(lambda: one.start())
+        sent_if.append((who, one))
+
     def tp_push(key, at, sems):
         ssem, rsem = sems
         for i, k in enumerate(tp_peers):
@@ -269,6 +305,7 @@
         pl.semaphore_signal(barrier, 1, device_id=tp_dev(k), device_id_type=MESH)
     for k in z_peers:
         pl.semaphore_signal(barrier, 1, device_id=z_dev(k), device_id_type=MESH)
+        pl.semaphore_signal(barrier, 1, device_id=(1 - c, k, t), device_id_type=MESH)
     load_x = load(0, x_hbm, r.xt.at[b])
     load_v = load(1, v_hbm, r.v)
     load_ids = load(2, ids_hbm, r.ids)
@@ -278,24 +315,33 @@
     load_s = load(6, squ_hbm, r.squ)
     load_x.wait()
     load_v.wait()
-    load_ids.wait()
-    r.xtf[t] = r.xt[b]
     r.vec[t, 0:12, :] = r.v[...]
     r.vec[t, 12:16, :] = jnp.zeros((4, G), f32)
+    pl.semaphore_wait(barrier, 1 + (ntp - 1) + 2 * (nb - 1))
+
+    if s.line:
+        inner = (b == 1) | (b == 2)
+        outer = (b == 0) | (b == 3)
+        for i in (1, 0):
+            j = z_peers[i]
+            push(("x", i), r.xt.at[b], r.xt.at[b], r.x_s.at[j], r.x_r.at[b], z_dev(j), r.xt.at[j], r.x_r.at[j])
+        j = z_peers[2]
+        push_if(inner, r.xt.at[b], r.xt.at[b], r.x_s.at[j], r.x_r.at[b], z_dev(j))
+        pending[("x", 2)] = copy(r.xt.at[j], r.xt.at[j], r.x_s.at[j], r.x_r.at[j], z_dev(j))
+    else:
+        for i, j in enumerate(z_peers):
+            push(("x", i), r.xt.at[b], r.xt.at[b], r.x_s.at[j], r.x_r.at[b], z_dev(j), r.xt.at[j], r.x_r.at[j])
+    for i, k in enumerate(tp_peers):
+        push(("xtf", i), r.xt.at[b], r.xtf.at[t], r.xtf_s.at[k], r.xtf_r.at[t], tp_dev(k), r.xtf.at[k], r.xtf_r.at[k])
+    tp_push("vec", lambda k: r.vec.at[k], sems(r.vec_s, r.vec_r))
     load_w.wait()
     w_ref = r.w
     w_o = w_ref[:, s.lo[2]:s.lo[2] + s.d].astype(bf16)
-    r.wo[...] = w_o
-    w_ot = flip(w_o).astype(bf16)
-    r.wot[t, 0] = w_ot[:s.d // 2]
-    r.wot[t, 1] = w_ot[s.d // 2:]
-    pl.semaphore_wait(barrier, 1 + (ntp - 1) + (nb - 1))
-
-    for i, j in enumerate(z_peers):
-        push(("x", i), r.xt.at[b], r.xt.at[b], r.x_s.at[j], r.x_r.at[b], z_dev(j), r.xt.at[j], r.x_r.at[j])
-    tp_push("vec", lambda k: r.vec.at[k], sems(r.vec_s, r.vec_r))
-    tp_push("xtf", lambda k: r.xtf.at[k], sems(r.xtf_s, r.xtf_r))
+    for h in range(2):
+        r.wot[t, h] = w_o[h * (G // 2):(h + 1) * (G // 2)]
     tp_push("wot", lambda k: r.wot.at[k, c], sems(r.wot_s, r.wot_r))
+    r.xtf[t] = r.xt[b]
+    load_ids.wait()
 
     w_q = w_ref[:, 0:G].astype(bf16)
     w_k = w_ref[:, G:2 * G].astype(bf16)
@@ -386,6 +432,17 @@
             r.vals[j] = (nn(x_j, r.wv[...]) + bias_v_row).astype(bf16)
 
     forward_block(b)
+    if s.line:
+        far = z_peers[1]
+        here = copy(r.xt.at[far], r.xt.at[far], r.x_s.at[far], r.x_r.at[far], z_dev(far))
+        on = copy(r.xt.at[far], r.xt.at[far], r.xf_s.at[0], r.x_r.at[far], z_dev(3 - far))
+
+        @pl.when(inner)
+        def _():
+            here.wait_recv()
+            on.start()
+
+        sent_if.append((inner, on))
 
     w_1 = w_ref[:, s.lo[1]:s.lo[1] + HG].astype(bf16)
     w_2 = w_ref[:, s.lo[0]:s.lo[0] + HG].astype(bf16)
@@ -396,6 +453,34 @@
     load_cot.wait()
     load_m.wait()
     load_s.wait()
+
+    def packed(a):
+        parts = [a[:, k * 128:(k + 1) * 128] for k in range(3 * G // 128)]
+        rest = a[:, 3 * G // 128 * 128:]
+        parts += [jnp.concatenate([rest[:G // 2], rest[G // 2:]], axis=1)]
+        parts += [jnp.zeros((s.pack - 3 * G * G // 128, 128), a.dtype)]
+        return jnp.concatenate(parts, axis=0)
+
+    def unpacked(a):
+        parts = [a[k * G:(k + 1) * G] for k in range(3 * G // 128)]
+        rest = a[3 * G // 128 * G:3 * G * G // 128]
+        parts += [jnp.concatenate([rest[:, :64], rest[:, 64:]], axis=0)]
+        return jnp.concatenate(parts, axis=1)
+
+    r.pw[...] = packed(w_ref[:, 0:3 * G])
+    r.pm[...] = packed(r.mom[:, 0:3 * G])
+    r.ps[...] = packed(r.squ[:, 0:3 * G])
+
+    def total(a):
+        return jnp.broadcast_to(jnp.sum(jnp.sum(a, axis=0, keepdims=True), axis=1, keepdims=True), (1, 128))
+
+    def columns(m):
+        return w_ref[:, s.lo[m]:s.lo[m] + s.width[m]]
+
+    lead = columns(3)
+    weight_sums = [total(a * a) for a in (lead[:, 0:G], lead[:, G:2 * G], lead[:, 2 * G:], columns(2), columns(1), columns(0))]
+    r.nrm[t] = jnp.concatenate(weight_sums + [jnp.zeros((2, 128), f32)], axis=0)
+    tp_push("nrm", lambda k: r.nrm.at[k], sems(r.nrm_s, r.nrm_r))
 
     def context_ready(k):
         r.lse[k] = r.mrun[k] + jnp.log(r.lrun[k])
@@ -410,7 +495,10 @@
 
     if s.keep:
         for i, j in enumerate(z_peers):
-            arrive(("x", i))
+            if s.line and i == 1:
+                pl.when(outer)(lambda: pending.pop(("x", 1)).wait_recv())
+            else:
+                arrive(("x", i))
             forward_block(j, context_ready if i == nb - 2 else None)
     else:
         def forward_remote(o, _):
@@ -425,16 +513,25 @@
         for k in range(nc):
             context_ready(k)
 
+    if s.keep:
+        for j in range(nb):
+            for k in range(nc):
+                r.ebuf[j, k] = (r.ebuf[j, k].astype(f32) * jnp.exp(r.mrec[j, k] - r.lse[k])).astype(bf16)
+
     tp_arrive("wot")
     for i, k in enumerate(tp_peers):
         push(("woc", i), r.wot.at[k, c], r.wot.at[k, c], r.woc_s.at[k], r.woc_r.at[k], core, r.wot.at[k, 1 - c], r.woc_r.at[k])
     tp_arrive("vec")
     tp_arrive("xtf")
+    tp_arrive("nrm")
     out_bias = [columns_of(r.vec[k])[:, 2:3] for k in range(ntp)]
     tp_arrive("woc")
+
+    def output_rows(k):
+        return jnp.concatenate([r.wot[k, 0], r.wot[k, 1]], axis=0)
+
     for k in range(ntp):
-        for h in range(2):
-            r.wof[h * (s.d // 2):(h + 1) * (s.d // 2), k * G:(k + 1) * G] = r.wot[k, h]
+        r.wof[:, k * G:(k + 1) * G] = flip(output_rows(k)).astype(bf16)
 
     gain1 = v_col(3)
     bias_rows = HG // G
@@ -512,45 +609,96 @@
     def sum_start(m):
         push(("gc", m), r.gsrc.at[m, 1 - c], r.gcore.at[m], r.gc_s.at[m], r.gc_r.at[m], core, r.gcore.at[m], r.gc_r.at[m])
 
+    def add_low(a, b):
+        return (a.astype(f32) + b.astype(f32)).astype(bf16)
+
     def when_owner(j, body):
         if s.owners < nb:
             pl.when(j < s.owners)(body)
         else:
             body()
 
+    def quarter(j):
+        return pl.ds(pl.multiple_of(j * s.rq, 16), s.rq)
+
     def to_owner(m, j):
-        return copy(r.ghalf.at[m, j], r.gz.at[m, b], r.gz_s.at[m, j], r.gz_r.at[m, b], z_dev(j))
+        return r.ghalf.at[m, quarter(j)], r.gz.at[m, b], r.gz_s.at[m, j], r.gz_r.at[m, b], z_dev(j)
 
     def to_all(m, j):
-        mine = r.gfin.at[m, c, b]
-        return copy(mine, mine, r.ga_s.at[m, j], r.ga_r.at[m, b], z_dev(j))
+        mine = r.gfin.at[m, c, quarter(b)]
+        return mine, mine, r.ga_s.at[m, j], r.ga_r.at[m, b], z_dev(j)
+
+    beside, across = (z_peers[0], z_peers[2]) if s.line else (None, None)
+
+    def landed(ref, sem, dev):
+        copy(ref, ref, sem, sem, dev).wait_recv()
 
     def sum_spread(m):
         arrive(("gc", m))
-        both = (r.gsrc[m, c].astype(f32) + r.gcore[m].astype(f32)).astype(bf16)
-        for k in range(s.owners):
-            r.ghalf[m, k] = both[k * s.rq:(k + 1) * s.rq]
-        for j in z_peers:
-            when_owner(j, lambda: to_owner(m, j).start())
+        r.ghalf[m] = add_low(r.gsrc[m, c], r.gcore[m])
+        if s.line:
+            push_if(outer, r.ghalf.at[m], r.gend.at[m], r.ge_s.at[m], r.ge_r.at[m], z_dev(beside))
+        else:
+            for j in z_peers:
+                when_owner(j, lambda: copy(*to_owner(m, j)).start())
+
+    def sum_cross(m):
+        if s.line:
+            one = copy(r.gmid.at[m], r.gcross.at[m], r.gx_s.at[m], r.gx_r.at[m], z_dev(across))
+
+            @pl.when(inner)
+            def _():
+                landed(r.gend.at[m], r.ge_r.at[m], z_dev(beside))
+                r.gmid[m] = add_low(r.ghalf[m], r.gend[m])
+                one.start()
+
+            sent_if.append((inner, one))
 
     def sum_own(m):
-        def body():
+        if s.line:
+            mine = r.gfin.at[m, c]
+            one = copy(mine, mine, r.ga_s.at[m, 0], r.ga_r.at[m, 0], z_dev(beside))
+
+            @pl.when(inner)
+            def _():
+                landed(r.gcross.at[m], r.gx_r.at[m], z_dev(across))
+                r.gfin[m, c] = add_low(r.gmid[m], r.gcross[m])
+                one.start()
+                r.upd[m:m + 1, :] = norm_of(m)
+
+            sent_if.append((inner, one))
+        else:
+            def body():
+                for j in z_peers:
+                    landed(r.gz.at[m, j], r.gz_r.at[m, j], z_dev(j))
+                r.gz[m, b] = r.ghalf[m, quarter(b)]
+                sums = r.gz[m, 0].astype(f32)
+                for j in range(1, nb):
+                    sums = sums + r.gz[m, j].astype(f32)
+                r.gfin[m, c, quarter(b)] = sums.astype(bf16)
+                for j in z_peers:
+                    copy(*to_all(m, j)).start()
+                r.upd[m:m + 1, :] = norm_of(m, b)
+
+            when_owner(b, body)
+
+    def norm_of(m, piece=None):
+        here = slice(None) if piece is None else quarter(piece)
+
+        def own_half(ref):
+            first, second = (ref[here, s.lo[m] + h * s.half:s.lo[m] + (h + 1) * s.half] for h in range(2))
+            return jnp.where(c == 0, first, second)
+
+        _, _, u = lamb_moments(r.gfin[m, c, here].astype(f32), own_half(r.mom), own_half(r.squ))
+        u = u + decay_rate * own_half(w_ref)
+        return total(u * u)
+
+    def sum_share(m):
+        if s.line:
+            pl.when(outer)(lambda: landed(r.gfin.at[m, c], r.ga_r.at[m, 0], z_dev(beside)))
+        else:
             for j in z_peers:
-                copy(r.gz.at[m, j], r.gz.at[m, j], r.gz_s.at[m, 0], r.gz_r.at[m, j], z_dev(j)).wait_recv()
-            r.gz[m, b] = r.ghalf[m, b]
-            total = r.gz[m, 0].astype(f32)
-            for j in range(1, nb):
-                total = total + r.gz[m, j].astype(f32)
-            r.gfin[m, c, b] = total.astype(bf16)
-            for j in z_peers:
-                to_all(m, j).start()
-
-        when_owner(b, body)
-
-    def sum_share(m):
-        for j in z_peers:
-            slot = r.gfin.at[m, c, j]
-            when_owner(j, lambda: copy(slot, slot, r.ga_s.at[m, 0], r.ga_r.at[m, j], z_dev(j)).wait_recv())
+                when_owner(j, lambda: landed(r.gfin.at[m, c, quarter(j)], r.ga_r.at[m, j], z_dev(j)))
         push(("gd", m), r.gfin.at[m, c], r.gfin.at[m, c], r.gd_s.at[m], r.gd_r.at[m], core, r.gfin.at[m, 1 - c], r.gd_r.at[m])
 
     def sum_done(m):
@@ -559,11 +707,11 @@
 
     def sum_sends_done(m):
         for j in z_peers:
-            when_owner(j, lambda: to_owner(m, j).wait_send())
+            when_owner(j, lambda: copy(*to_owner(m, j)).wait_send())
 
         def body():
             for j in z_peers:
-                to_all(m, j).wait_send()
+                copy(*to_all(m, j)).wait_send()
 
         when_owner(b, body)
 
@@ -585,6 +733,10 @@
     vgl[5 + bias_rows:6 + bias_rows, :] = lane_sums(r.dffn[...])
     vgl[6 + bias_rows:7 + bias_rows, :] = lane_sums_f32(r.cn2[...])
     vgl[7 + bias_rows:8 + bias_rows, :] = lane_sums(r.cot[...])
+    r.upd[...] = jnp.zeros((8, 128), f32)
+    if s.line:
+        sum_spread(0)
+        sum_spread(1)
 
     def context_chunk(k):
         tp_arrive(("st2", k))
@@ -599,7 +751,7 @@
             rows = slice(d * G, (d + 1) * G)
             part = inv * (r.dmgg[k, rows, :].astype(f32) - first - r.n1f[k, rows, :] * second)
             r.datt[rows, lanes(k)] = part.astype(bf16)
-        dctx = nn(r.wo[...], r.datt[:, lanes(k)]).astype(bf16).astype(f32)
+        dctx = nn(output_rows(t), r.datt[:, lanes(k)]).astype(bf16).astype(f32)
         r.dcz[k] = by_head(dctx)
         parts = [
             jnp.sum(dctx[head_rows(h)] * r.acc[head_rows(h), lanes(k)], axis=0, keepdims=True)
@@ -623,14 +775,15 @@
         dk = dv = None
         for k in chunks:
             if s.keep:
-                p = r.ebuf[j, k].astype(f32) * jnp.exp(r.mrec[j, k] - r.lse[k])
+                p_low = r.ebuf[j, k]
+                p = p_low.astype(f32)
             else:
                 p = jnp.exp(jnp.where(same_doc(j, k), nn(keys, r.qz[k]), NEG) - r.lse[k])
+                p_low = p.astype(bf16)
             ds = (p * (nn(vals, r.dcz[k]) - r.delta[k])).astype(bf16)
-            p = p.astype(bf16)
             for h in range(s.heads):
                 r.dqt[head_rows(h), lanes(k)] += nn(keys_t[head_rows(h), :], ds[:, lanes(h)])
-            dk_k, dv_k = nt(ds, r.qz[k]), nt(p, r.dcz[k])
+            dk_k, dv_k = nt(ds, r.qz[k]), nt(p_low, r.dcz[k])
             dk, dv = (dk_k, dv_k) if dk is None else (dk + dk_k, dv + dv_k)
         return dk, dv
 
@@ -643,12 +796,10 @@
         return nt(r.wk[...], dk) + nt(r.wv[...], dv)
 
     def dx_send(j):
-        return copy(r.dxs.at[j], r.dxr.at[b], r.dx_s.at[j], r.dx_r.at[b], z_dev(j))
+        return r.dxs.at[j], r.dxr.at[b], r.dx_s.at[j], r.dx_r.at[b], z_dev(j)
 
     if s.keep:
         context_chunk(0)
-        sum_spread(0)
-        sum_spread(1)
         for j in z_peers + [b]:
             r.dkb[j], r.dvb[j] = pair_terms(j, [0])
         for k in range(1, nc):
@@ -656,17 +807,19 @@
         keep_grad(2, nt(r.ctxl[...], r.datt[...]))
         sum_start(2)
         vgl[2:3, :] = lane_sums(r.dxo[...].astype(bf16))
-        sum_own(0)
-        sum_own(1)
-        for i, j in enumerate(z_peers):
+        for i in (1, 2, 0):
+            j = z_peers[i]
             dk, dv = pair_terms(j, range(1, nc))
             r.dxs[j] = finish_block(j, dk + r.dkb[j], dv + r.dvb[j]).astype(bf16)
-            dx_send(j).start()
             if i == 0:
-                sum_spread(2)
-            if i == nb - 2:
-                sum_share(0)
-                sum_share(1)
+                push(("dx", 0), *dx_send(j), r.dxr.at[j], r.dx_r.at[j])
+                sum_cross(1)
+            else:
+                push_if(outer, r.dxs.at[j], r.dxa.at[j], r.da_s.at[j], r.da_r.at[j], z_dev(beside))
+                if i == 1:
+                    sum_spread(2)
+                else:
+                    sum_cross(0)
         dk, dv = pair_terms(b, range(1, nc))
         r.dxo[...] += finish_block(b, dk + r.dkb[b], dv + r.dvb[b])
     else:
@@ -679,7 +832,7 @@
         def backward_remote(o, _):
             j = (b + o) % nb
             r.dxs[j] = finish_block(j, *pair_terms(j, range(nc))).astype(bf16)
-            dx_send(j).start()
+            copy(*dx_send(j)).start()
             return 0
 
         lax.fori_loop(1, nb, backward_remote, 0)
@@ -688,55 +841,114 @@
             sum_spread(m)
         sum_own(0)
         sum_own(1)
-        sum_share(0)
-        sum_share(1)
     dq_t = (r.dqt[...] * scaling).astype(bf16)
-    r.gsrc[3, 0, :, 0:G] = nt(r.xt[b], dq_t).astype(bf16)
-    r.gsrc[3, 0, :, G:2 * G] = r.gkv[0].astype(bf16)
-    r.gsrc[3, 1, :, 0:G] = r.gkv[1].astype(bf16)
-    r.gsrc[3, 1, :, G:2 * G] = jnp.zeros((G, G), bf16)
-    sum_start(3)
+    r.qsrc[...] = packed(jnp.concatenate([nt(r.xt[b], dq_t), r.gkv[0], r.gkv[1]], axis=1)).astype(bf16)
+
+    def part(k, n):
+        return pl.ds(pl.multiple_of(k * n, 16), n)
+
+    push("qc", r.qsrc.at[part(1 - c, s.ph)], r.qcore, r.qc_s.at[0], r.qc_r.at[0], core, r.qcore, r.qc_r.at[0])
     vgl[0:1, :] = lane_sums(dq_t)
     vgl[1:2, :] = r.vb[...]
-    push(("vc",), vgl, r.vgc, r.vc_s.at[0], r.vc_r.at[0], core, r.vgc, r.vc_r.at[0])
-    sum_spread(3)
-    arrive(("vc",))
+    push("vc", vgl, r.vgc, r.vc_s.at[0], r.vc_r.at[0], core, r.vgc, r.vc_r.at[0])
+    arrive("qc")
+    r.qhalf[...] = add_low(r.qsrc[part(c, s.ph)], r.qcore[...])
+
+    def q_to_owner(j):
+        return r.qhalf.at[part(j, s.pr)], r.qz_in.at[b], r.qz_s.at[j], r.qz_r.at[b], z_dev(j)
+
+    def q_to_all(j):
+        mine = r.qfin.at[part(c * s.owners + b, s.pr)]
+        return mine, mine, r.qa_s.at[j], r.qa_r.at[b], z_dev(j)
+
+    for j in z_peers:
+        when_owner(j, lambda: copy(*q_to_owner(j)).start())
+    arrive("vc")
     r.vgs[...] = vgl[...] + r.vgc[...]
     r.vgz[b] = r.vgs[...]
     for i, j in enumerate(z_peers):
         push(("vz", i), r.vgs, r.vgz.at[b], r.vz_s.at[j], r.vz_r.at[b], z_dev(j), r.vgz.at[j], r.vz_r.at[j])
+    if s.line:
+        sum_own(0)
+        sum_cross(2)
+        sum_own(1)
+
+        @pl.when(inner)
+        def _():
+            for i in (1, 2):
+                j = z_peers[i]
+                landed(r.dxa.at[j], r.da_r.at[j], z_dev(beside))
+                r.dxs[j] = add_low(r.dxs[j], r.dxa[j])
+                copy(*dx_send(j)).start()
+
+        for i in (1, 2):
+            sent_if.append((inner, copy(*dx_send(z_peers[i]))))
+    else:
+        sum_own(2)
     r.dxo[...] += nn(r.wq[...], dq_t)
-    sum_own(2)
-
-    def norms_of(m):
-        rows = []
-        for h in range(2):
-            lo = s.lo[m] + h * s.half
-            wide = min(s.half, s.lo[m] + s.width[m] - lo)
-            grad = jnp.concatenate([r.gfin[m, h, k] for k in range(s.owners)], axis=0)[:, :wide]
-            w = w_ref[:, lo:lo + wide]
-            _, _, u = lamb_moments(grad.astype(f32), r.mom[:, lo:lo + wide], r.squ[:, lo:lo + wide])
-            u = u + decay_rate * w
-            rows.append((jnp.sum(w * w, axis=0, keepdims=True), jnp.sum(u * u, axis=0, keepdims=True)))
-        return rows
-
-    def total(a):
-        return jnp.broadcast_to(jnp.sum(a, axis=1, keepdims=True), (1, 128))
-
-    sums = {}
-    for m in (0, 1):
-        sum_done(m)
-        sums[m] = norms_of(m)
-    sum_own(3)
-    sum_share(2)
-    for i, j in enumerate(z_peers):
-        copy(r.dxr.at[j], r.dxr.at[j], r.dx_s.at[j], r.dx_r.at[j], z_dev(j)).wait_recv()
-        r.dxo[...] += r.dxr[j].astype(f32)
+
+    mine = jnp.zeros((s.pr, 128), f32)
+    for j in z_peers:
+        when_owner(b, lambda: landed(r.qz_in.at[j], r.qz_r.at[j], z_dev(j)))
+    r.qz_in[b] = r.qhalf[part(b % s.owners, s.pr)]
+    for j in range(nb):
+        mine = mine + r.qz_in[j].astype(f32)
+    mine = mine.astype(bf16)
+
+    @partial(when_owner, b)
+    def _():
+        r.qfin[part(c * s.owners + b, s.pr), :] = mine
+        for j in z_peers:
+            copy(*q_to_all(j)).start()
+
+    first_row = (c * s.owners + b % s.owners) * s.pr
+    here = part(c * s.owners + b % s.owners, s.pr)
+    _, _, u = lamb_moments(mine.astype(f32), r.pm[here, :], r.ps[here, :])
+    u = u + decay_rate * r.pw[here, :]
+    u = jnp.where(b < s.owners, u * u, 0.0)
+    row = first_row + lax.broadcasted_iota(jnp.int32, (s.pr, 128), 0)
+    lane = lax.broadcasted_iota(jnp.int32, (s.pr, 128), 1)
+    column = row // G * 128 + lane
+    is_q = column < G
+    is_k = (column >= G) & (column < 2 * G)
+    is_v = column >= 2 * G
+    lead = [total(jnp.where(a, u, 0.0)) for a in (is_q, is_k, is_v)]
+    if s.line:
+        sum_own(2)
+        rest = jnp.where(b == 1, r.upd[...], 0.0)
+    else:
+        rest = r.upd[...]
+    r.nq[c, b] = jnp.concatenate(lead + [rest[m:m + 1] for m in (2, 1, 0)] + [jnp.zeros((2, 128), f32)], axis=0)
+    same_tp = [(1 - c, b)] + [(i, j) for j in z_peers for i in (c, 1 - c)]
+    for n, (i, j) in enumerate(same_tp):
+        push(("nq", n), r.nq.at[c, b], r.nq.at[c, b], r.nq_s.at[i, j], r.nq_r.at[c, b], (i, j, t), r.nq.at[i, j], r.nq_r.at[i, j])
+    sum_share(0)
+    sum_share(1)
+    if s.line:
+        other = jnp.where(b < 2, 2, 1)
+        arrive(("dx", 0))
+        landed(r.dxr.at[other], r.dx_r.at[other], z_dev(other))
+        r.dxo[...] += r.dxr[beside].astype(f32) + r.dxr[other].astype(f32)
+    else:
+        for j in z_peers:
+            landed(r.dxr.at[j], r.dx_r.at[j], z_dev(j))
+            r.dxo[...] += r.dxr[j].astype(f32)
     ig_ref[...] = r.dxo[...]
     store(ig_ref, ig_hbm)
-    sum_done(2)
-    sums[2] = norms_of(2)
-    sum_share(3)
+    sum_share(2)
+    for n in range(len(same_tp)):
+        arrive(("nq", n))
+    sums = jnp.zeros((8, 128), f32)
+    for i in range(s.nr):
+        for j in range(nb):
+            sums = sums + r.nq[i, j]
+    r.nqt[t] = sums
+    tp_push("nqt", lambda k: r.nqt.at[k], sems(r.nqt_s, r.nqt_r))
+    for j in z_peers:
+        when_owner(j, lambda: landed(r.qfin.at[part(c * s.owners + j, s.pr)], r.qa_r.at[j], z_dev(j)))
+    push("qd", r.qfin.at[part(c, s.ph)], r.qfin.at[part(c, s.ph)], r.qd_s.at[0], r.qd_r.at[0], core, r.qfin.at[part(1 - c, s.ph)], r.qd_r.at[0])
+    for m in range(3):
+        sum_done(m)
     for i in range(nb - 1):
         arrive(("vz", i))
     vg = r.vgz[0]
@@ -744,29 +956,38 @@
         vg = vg + r.vgz[j]
     vg_ref[...] = vg[0:12]
     store(vg_ref, vg_hbm)
-    sum_done(3)
-    sums[3] = norms_of(3)
-    packed = []
-    for which in range(2):
-        lead = sums[3][0][which]
-        packed += [total(lead[:, 0:G]), total(lead[:, G:2 * G]), total(sums[3][1][which])]
-        packed += [total(sums[m][0][which] + sums[m][1][which]) for m in (2, 1, 0)]
-        packed += [jnp.zeros((2, 128), f32)]
-    r.nrm[t] = jnp.concatenate(packed, axis=0)
-    tp_push("nrm", lambda k: r.nrm.at[k], sems(r.nrm_s, r.nrm_r))
-    tp_arrive("nrm")
+    arrive("qd")
+    lead = unpacked(r.qfin[...])
+    r.gq[0] = lead[:, 0:s.half]
+    r.gq[1, :, 0:G] = lead[:, s.half:]
+    r.gq[1, :, G:2 * G] = jnp.zeros((G, G), bf16)
+    store(r.gq, g_hbm.at[3])
+    tp_arrive("nqt")
     norms = r.nrm[0]
+    lead = r.nqt[0]
     for k in range(1, ntp):
         norms = norms + r.nrm[k]
-    ratio_ref[...] = jnp.sqrt(norms[0:8] / (norms[8:16] + 1e-12))
+        lead = lead + r.nqt[k]
+    ratio_ref[...] = jnp.sqrt(norms / (lead + 1e-12))
     store(ratio_ref, ratio_hbm)
 
     for one in sent:
         one.wait_send()
-    for m in range(4):
-        sum_sends_done(m)
+    for who, one in sent_if:
+        pl.when(who)(lambda: one.wait_send())
+    if not s.line:
+        for m in range(3):
+            sum_sends_done(m)
+        for j in z_peers:
+            copy(*dx_send(j)).wait_send()
     for j in z_peers:
-        dx_send(j).wait_send()
+        when_owner(j, lambda: copy(*q_to_owner(j)).wait_send())
+
+    @partial(when_owner, b)
+    def _():
+        for j in z_peers:
+            copy(*q_to_all(j)).wait_send()
+
     for one in stored:
         one.wait()
 
@@ -779,7 +1000,7 @@
         for h in range(2):
             lo = s.lo[m] + h * s.half
             wide = min(s.half, s.lo[m] + s.width[m] - lo)
-            grad[:, lo:lo + wide] = g_ref[m, h, 0, :, 0:wide].astype(f32)
+            grad[:, lo:lo + wide] = g_ref[m, h, :, 0:wide].astype(f32)
     cols = s.cols
     g = grad[...]
     gm_ref[...] = g
@@ -820,7 +1041,7 @@
         out_shape=(
             S(tokens.shape, bf16),
             S(tokens.shape, f32),
-            S((4, 2, s.owners, s.rq, s.half), bf16),
+            S((4, 2, s.g, s.half), bf16),
             S(vectors.shape, f32),
             S((8, 128), f32),
         ),
@@ -860,7 +1081,7 @@
         ),
         in_specs=[
             rows(tokens, s.rq), rows(tokens, s.rq), mat, mat, mat,
-            pl.BlockSpec((4, 2, 1, s.rq, s.half), lambda i: (0, 0, i, 0, 0)),
+            pl.BlockSpec((4, 2, s.rq, s.half), lambda i: (0, 0, i, 0)),
             pl.BlockSpec((8, 128), lambda i: (0, 0)), vec, vec, vec, vec,
         ],
         out_specs=(rows(tokens, s.rq), rows(tokens, s.rq), mat, vec, mat, mat, vec, vec, mat, vec),

time: 92.7 us -> 79.1 us (0.85)
  Pallas kernels: 91.7 us -> 78 us
    pallas_call x1, Pallas kernels: 86.7 us -> 73 us  [local(): pl.pallas_call(partial(layer_kernel, s, names), out_shape=(S(tokens.shape...]
where the time goes in v3:
time: 79.1 us; the launch traced here: 78.9 us
  Pallas kernels  78 us (99%)
  between operations  0.91 us (1%)
    pallas_call x1, Pallas kernels, local(): pl.pallas_call(partial(layer_kernel, s, names), out_shape=(S(tokens.shape...  73 us
    pallas_call x1, Pallas kernels, local(): pl.pallas_call(partial(finish_kernel, s), grid=(steps,), out_shape=(S(tok...  4.97 us

profile of v3, /device:TPU:0, one launch (start us, length us, event | category | flops | bytes accessed | tf_op | source)
XLA Modules:
  0.0 78.9 jit_solution(2806815183412597324)
XLA Ops:
  0.6 0.0 copy-start
  0.7 0.0 copy-start.1
  0.7 0.0 copy-start.2
  0.7 0.0 copy-start.3
  0.7 0.0 copy-start.4
  0.7 0.0 copy-start.5
  0.7 73.0 %layer.1 = (bf16[192,384]{1,0:T(8,128)(2,1)S(1)}, f32[192,384]{1,0:T(8,128)S(1)}, bf16[4,2,192,384]{3,2,1,0:T(8,128)(2,1)S(1)}, f32[12,192]{1,0:T(8,128)S(1)}, f32[8,128]{1,0:T(8,128)S(1)}) custom-call(bf16[192,384]{1,0:T(8,128)(2,1)} %bitcast.4, bf16[192,384]{1,0:T(8,128)(2,1)} %bitcast.5, s32[1,1536]{1,0:T(1,128)} %ids_hbm.1, f32[192,2880]{1,0:T(8,128)} %w_ref.1, ...), custom_call_target="tpu_custom_call" | custom-call | tf_op jit(solution)/shard_map/layer/pallas_call | solution.py:1039
  73.7 0.0 copy-done
  73.7 0.0 copy-done.1
  73.8 0.0 copy-done.2
  73.8 0.0 copy-done.3
  73.8 0.0 copy-done.4
  73.8 0.0 copy-done.5
  73.8 5.0 %finish.1 = (bf16[192,384]{1,0:T(8,128)(2,1)}, f32[192,384]{1,0:T(8,128)}, f32[192,2880]{1,0:T(8,128)}, f32[12,192]{1,0:T(8,128)}, f32[192,2880]{1,0:T(8,128)}, ...) custom-call(bf16[192,384]{1,0:T(8,128)(2,1)S(1)} %get-tuple-element., ...), custom_call_target="tpu_custom_call" | custom-call | tf_op jit(solution)/shard_map/finish/pallas_call | solution.py:1067
Async XLA Ops:
  0.6 73.1 %copy-start = (f32[192,2880]{1,0:T(8,128)S(1)}, f32[192,2880]{1,0:T(8,128)}, u32[]{:S(2)}) copy-start(f32[192,2880]{1,0:T(8,128)} %w_ref.1) | copy-start | bytes 6635524
  0.7 73.1 %copy-start.1 = (f32[192,2880]{1,0:T(8,128)S(1)}, f32[192,2880]{1,0:T(8,128)}, u32[]{:S(2)}) copy-start(f32[192,2880]{1,0:T(8,128)} %mom_ref.1) | copy-start | bytes 6635524
  0.7 73.1 %copy-start.2 = (f32[192,2880]{1,0:T(8,128)S(1)}, f32[192,2880]{1,0:T(8,128)}, u32[]{:S(2)}) copy-start(f32[192,2880]{1,0:T(8,128)} %squ_ref.1) | copy-start | bytes 6635524
  0.7 73.1 %copy-start.3 = (f32[12,192]{1,0:T(8,128)S(1)}, f32[12,192]{1,0:T(8,128)}, u32[]{:S(2)}) copy-start(f32[12,192]{1,0:T(8,128)} %v_ref.1) | copy-start | bytes 27652
  0.7 73.1 %copy-start.4 = (f32[12,192]{1,0:T(8,128)S(1)}, f32[12,192]{1,0:T(8,128)}, u32[]{:S(2)}) copy-start(f32[12,192]{1,0:T(8,128)} %mv_ref.1) | copy-start | bytes 27652
  0.7 73.1 %copy-start.5 = (f32[12,192]{1,0:T(8,128)S(1)}, f32[12,192]{1,0:T(8,128)}, u32[]{:S(2)}) copy-start(f32[12,192]{1,0:T(8,128)} %sv_ref.1) | copy-start | bytes 27652

commit v4 on v3

--- a/solution.py
+++ b/solution.py
@@ -24,6 +24,7 @@
 learn_rate = 0.04
 matrix_rate = 1.0
 NEG = -1e30
+RELAY = 0
 
 
 def nn(a, b):
@@ -201,6 +202,8 @@
         xtf_s=D((ntp,)), xtf_r=D((ntp,)),
         wot_s=D((ntp,)), wot_r=D((ntp,)),
         woc_s=D((ntp,)), woc_r=D((ntp,)),
+        xth_s=D((2,)), xth_r=D((2,)),
+        woh_s=D((2,)), woh_r=D((2,)),
         vec_s=D((ntp,)), vec_r=D((ntp,)),
         ctx_s=D((nc, ntp)), ctx_r=D((nc, ntp)),
         st1_s=D((nc, ntp)), st1_r=D((nc, ntp)),
@@ -331,7 +334,7 @@
     else:
         for i, j in enumerate(z_peers):
             push(("x", i), r.xt.at[b], r.xt.at[b], r.x_s.at[j], r.x_r.at[b], z_dev(j), r.xt.at[j], r.x_r.at[j])
-    for i, k in enumerate(tp_peers):
+    for i, k in enumerate(tp_peers[:2]):
         push(("xtf", i), r.xt.at[b], r.xtf.at[t], r.xtf_s.at[k], r.xtf_r.at[t], tp_dev(k), r.xtf.at[k], r.xtf_r.at[k])
     tp_push("vec", lambda k: r.vec.at[k], sems(r.vec_s, r.vec_r))
     load_w.wait()
@@ -339,7 +342,8 @@
     w_o = w_ref[:, s.lo[2]:s.lo[2] + s.d].astype(bf16)
     for h in range(2):
         r.wot[t, h] = w_o[h * (G // 2):(h + 1) * (G // 2)]
-    tp_push("wot", lambda k: r.wot.at[k, c], sems(r.wot_s, r.wot_r))
+    for i, k in enumerate(tp_peers[:2]):
+        push(("wot", i), r.wot.at[t, c], r.wot.at[t, c], r.wot_s.at[k], r.wot_r.at[t], tp_dev(k), r.wot.at[k, c], r.wot_r.at[k])
     r.xtf[t] = r.xt[b]
     load_ids.wait()
 
@@ -482,6 +486,21 @@
     r.nrm[t] = jnp.concatenate(weight_sums + [jnp.zeros((2, 128), f32)], axis=0)
     tp_push("nrm", lambda k: r.nrm.at[k], sems(r.nrm_s, r.nrm_r))
 
+    def half_rows(ref, h):
+        n = ref.shape[0] // 2
+        return ref.at[pl.ds(h * n, n)]
+
+    def relay(key, at, leaving, landing):
+        for h in range(2):
+            arrive((key, h))
+            block = half_rows(at(tp_peers[h]), h)
+            here = half_rows(at(tp_peers[2]), h)
+            push((key, 2 + h), block, block, leaving.at[h], landing.at[h], tp_dev(tp_peers[1 - h]), here, landing.at[h])
+
+    def relays():
+        relay("xtf", lambda k: r.xtf.at[k], r.xth_s, r.xth_r)
+        relay("wot", lambda k: r.wot.at[k, c], r.woh_s, r.woh_r)
+
     def context_ready(k):
         r.lse[k] = r.mrun[k] + jnp.log(r.lrun[k])
         inverse = 1.0 / r.lrun[k]
@@ -500,6 +519,8 @@
             else:
                 arrive(("x", i))
             forward_block(j, context_ready if i == nb - 2 else None)
+            if i == RELAY:
+                relays()
     else:
         def forward_remote(o, _):
             j = (b + o) % nb
@@ -507,6 +528,7 @@
             forward_block(j)
             return 0
 
+        relays()
         lax.fori_loop(1, nb, forward_remote, 0)
         for i in range(nb - 1):
             pending.pop(("x", i))
@@ -518,11 +540,13 @@
             for k in range(nc):
                 r.ebuf[j, k] = (r.ebuf[j, k].astype(f32) * jnp.exp(r.mrec[j, k] - r.lse[k])).astype(bf16)
 
-    tp_arrive("wot")
+    for h in range(2):
+        arrive(("wot", 2 + h))
     for i, k in enumerate(tp_peers):
         push(("woc", i), r.wot.at[k, c], r.wot.at[k, c], r.woc_s.at[k], r.woc_r.at[k], core, r.wot.at[k, 1 - c], r.woc_r.at[k])
     tp_arrive("vec")
-    tp_arrive("xtf")
+    for h in range(2):
+        arrive(("xtf", 2 + h))
     tp_arrive("nrm")
     out_bias = [columns_of(r.vec[k])[:, 2:3] for k in range(ntp)]
     tp_arrive("woc")
@@ -664,7 +688,6 @@
                 landed(r.gcross.at[m], r.gx_r.at[m], z_dev(across))
                 r.gfin[m, c] = add_low(r.gmid[m], r.gcross[m])
                 one.start()
-                r.upd[m:m + 1, :] = norm_of(m)
 
             sent_if.append((inner, one))
         else:
@@ -692,6 +715,12 @@
         _, _, u = lamb_moments(r.gfin[m, c, here].astype(f32), own_half(r.mom), own_half(r.squ))
         u = u + decay_rate * own_half(w_ref)
         return total(u * u)
+
+    def sum_norm(m):
+        if s.line:
+            @pl.when(inner)
+            def _():
+                r.upd[m:m + 1, :] = norm_of(m)
 
     def sum_share(m):
         if s.line:
@@ -863,11 +892,6 @@
 
     for j in z_peers:
         when_owner(j, lambda: copy(*q_to_owner(j)).start())
-    arrive("vc")
-    r.vgs[...] = vgl[...] + r.vgc[...]
-    r.vgz[b] = r.vgs[...]
-    for i, j in enumerate(z_peers):
-        push(("vz", i), r.vgs, r.vgz.at[b], r.vz_s.at[j], r.vz_r.at[b], z_dev(j), r.vgz.at[j], r.vz_r.at[j])
     if s.line:
         sum_own(0)
         sum_cross(2)
@@ -886,6 +910,8 @@
     else:
         sum_own(2)
     r.dxo[...] += nn(r.wq[...], dq_t)
+    sum_norm(0)
+    sum_norm(1)
 
     mine = jnp.zeros((s.pr, 128), f32)
     for j in z_peers:
@@ -915,6 +941,7 @@
     lead = [total(jnp.where(a, u, 0.0)) for a in (is_q, is_k, is_v)]
     if s.line:
         sum_own(2)
+        sum_norm(2)
         rest = jnp.where(b == 1, r.upd[...], 0.0)
     else:
         rest = r.upd[...]
@@ -922,6 +949,11 @@
     same_tp = [(1 - c, b)] + [(i, j) for j in z_peers for i in (c, 1 - c)]
     for n, (i, j) in enumerate(same_tp):
         push(("nq", n), r.nq.at[c, b], r.nq.at[c, b], r.nq_s.at[i, j], r.nq_r.at[c, b], (i, j, t), r.nq.at[i, j], r.nq_r.at[i, j])
+    arrive("vc")
+    r.vgs[...] = vgl[...] + r.vgc[...]
+    r.vgz[b] = r.vgs[...]
+    for i, j in enumerate(z_peers):
+        push(("vz", i), r.vgs, r.vgz.at[b], r.vz_s.at[j], r.vz_r.at[b], z_dev(j), r.vgz.at[j], r.vz_r.at[j])
     sum_share(0)
     sum_share(1)
     if s.line:

time: 79.1 us -> 78.4 us (level)
  no operation moved by 1% of the time
where the time goes in v4:
time: 78.4 us; the launch traced here: 78.2 us
  Pallas kernels  77.3 us (99%)
  between operations  0.91 us (1%)
    pallas_call x1, Pallas kernels, local(): pl.pallas_call(partial(layer_kernel, s, names), out_shape=(S(tokens.shape...  72.3 us
    pallas_call x1, Pallas kernels, local(): pl.pallas_call(partial(finish_kernel, s), grid=(steps,), out_shape=(S(tok...  4.97 us

profile of v4, /device:TPU:0, one launch (start us, length us, event | category | flops | bytes accessed | tf_op | source)
XLA Modules:
  0.0 78.2 jit_solution(2462982713939964586)
XLA Ops:
  0.6 0.0 copy-start
  0.7 0.0 copy-start.1
  0.7 0.0 copy-start.2
  0.7 0.0 copy-start.3
  0.7 0.0 copy-start.4
  0.7 0.0 copy-start.5
  0.7 72.3 %layer.1 = (bf16[192,384]{1,0:T(8,128)(2,1)S(1)}, f32[192,384]{1,0:T(8,128)S(1)}, bf16[4,2,192,384]{3,2,1,0:T(8,128)(2,1)S(1)}, f32[12,192]{1,0:T(8,128)S(1)}, f32[8,128]{1,0:T(8,128)S(1)}) custom-call(bf16[192,384]{1,0:T(8,128)(2,1)} %bitcast.4, bf16[192,384]{1,0:T(8,128)(2,1)} %bitcast.5, s32[1,1536]{1,0:T(1,128)} %ids_hbm.1, f32[192,2880]{1,0:T(8,128)} %w_ref.1, ...), custom_call_target="tpu_custom_call" | custom-call | tf_op jit(solution)/shard_map/layer/pallas_call | solution.py:1071
  73.0 0.0 copy-done
  73.0 0.0 copy-done.1
  73.0 0.0 copy-done.2
  73.0 0.0 copy-done.3
  73.0 0.0 copy-done.4
  73.1 0.0 copy-done.5
  73.1 5.0 %finish.1 = (bf16[192,384]{1,0:T(8,128)(2,1)}, f32[192,384]{1,0:T(8,128)}, f32[192,2880]{1,0:T(8,128)}, f32[12,192]{1,0:T(8,128)}, f32[192,2880]{1,0:T(8,128)}, ...) custom-call(bf16[192,384]{1,0:T(8,128)(2,1)S(1)} %get-tuple-element., ...), custom_call_target="tpu_custom_call" | custom-call | tf_op jit(solution)/shard_map/finish/pallas_call | solution.py:1099
Async XLA Ops:
  0.6 72.4 %copy-start = (f32[192,2880]{1,0:T(8,128)S(1)}, f32[192,2880]{1,0:T(8,128)}, u32[]{:S(2)}) copy-start(f32[192,2880]{1,0:T(8,128)} %w_ref.1) | copy-start | bytes 6635524
  0.7 72.4 %copy-start.1 = (f32[192,2880]{1,0:T(8,128)S(1)}, f32[192,2880]{1,0:T(8,128)}, u32[]{:S(2)}) copy-start(f32[192,2880]{1,0:T(8,128)} %mom_ref.1) | copy-start | bytes 6635524
  0.7 72.4 %copy-start.2 = (f32[192,2880]{1,0:T(8,128)S(1)}, f32[192,2880]{1,0:T(8,128)}, u32[]{:S(2)}) copy-start(f32[192,2880]{1,0:T(8,128)} %squ_ref.1) | copy-start | bytes 6635524
  0.7 72.4 %copy-start.3 = (f32[12,192]{1,0:T(8,128)S(1)}, f32[12,192]{1,0:T(8,128)}, u32[]{:S(2)}) copy-start(f32[12,192]{1,0:T(8,128)} %v_ref.1) | copy-start | bytes 27652
  0.7 72.4 %copy-start.4 = (f32[12,192]{1,0:T(8,128)S(1)}, f32[12,192]{1,0:T(8,128)}, u32[]{:S(2)}) copy-start(f32[12,192]{1,0:T(8,128)} %mv_ref.1) | copy-start | bytes 27652
  0.7 72.4 %copy-start.5 = (f32[12,192]{1,0:T(8,128)S(1)}, f32[12,192]{1,0:T(8,128)}, u32[]{:S(2)}) copy-start(f32[12,192]{1,0:T(8,128)} %sv_ref.1) | copy-start | bytes 27652

commit v5 on v4

--- a/solution.py
+++ b/solution.py
@@ -277,7 +277,7 @@
 
     def tp_push(key, at, sems):
         ssem, rsem = sems
-        for i, k in enumerate(tp_peers):
+        for i, k in reversed(list(enumerate(tp_peers))):
             push((key, i), at(t), at(t), ssem(k), rsem(t), tp_dev(k), at(k), rsem(k))
 
     def tp_arrive(key):
@@ -890,7 +890,7 @@
         mine = r.qfin.at[part(c * s.owners + b, s.pr)]
         return mine, mine, r.qa_s.at[j], r.qa_r.at[b], z_dev(j)
 
-    for j in z_peers:
+    for j in reversed(z_peers):
         when_owner(j, lambda: copy(*q_to_owner(j)).start())
     if s.line:
         sum_own(0)
@@ -924,7 +924,7 @@
     @partial(when_owner, b)
     def _():
         r.qfin[part(c * s.owners + b, s.pr), :] = mine
-        for j in z_peers:
+        for j in reversed(z_peers):
             copy(*q_to_all(j)).start()
 
     first_row = (c * s.owners + b % s.owners) * s.pr

time: 78.4 us -> 78.1 us (level)
  no operation moved by 1% of the time
where the time goes in v5:
time: 78.1 us; the launch traced here: 78 us
  Pallas kernels  77 us (99%)
  between operations  0.91 us (1%)
    pallas_call x1, Pallas kernels, local(): pl.pallas_call(partial(layer_kernel, s, names), out_shape=(S(tokens.shape...  72.1 us
    pallas_call x1, Pallas kernels, local(): pl.pallas_call(partial(finish_kernel, s), grid=(steps,), out_shape=(S(tok...  4.97 us

profile of v5, /device:TPU:0, one launch (start us, length us, event | category | flops | bytes accessed | tf_op | source)
XLA Modules:
  0.0 78.0 jit_solution(5428992110704644387)
XLA Ops:
  0.6 0.0 copy-start
  0.7 0.0 copy-start.1
  0.7 0.0 copy-start.2
  0.7 0.0 copy-start.3
  0.7 0.0 copy-start.4
  0.7 0.0 copy-start.5
  0.7 72.1 %layer.1 = (bf16[192,384]{1,0:T(8,128)(2,1)S(1)}, f32[192,384]{1,0:T(8,128)S(1)}, bf16[4,2,192,384]{3,2,1,0:T(8,128)(2,1)S(1)}, f32[12,192]{1,0:T(8,128)S(1)}, f32[8,128]{1,0:T(8,128)S(1)}) custom-call(bf16[192,384]{1,0:T(8,128)(2,1)} %bitcast.4, bf16[192,384]{1,0:T(8,128)(2,1)} %bitcast.5, s32[1,1536]{1,0:T(1,128)} %ids_hbm.1, f32[192,2880]{1,0:T(8,128)} %w_ref.1, ...), custom_call_target="tpu_custom_call" | custom-call | tf_op jit(solution)/shard_map/layer/pallas_call | solution.py:1071
  72.8 0.0 copy-done
  72.8 0.0 copy-done.1
  72.8 0.0 copy-done.2
  72.8 0.0 copy-done.3
  72.8 0.0 copy-done.4
  72.8 0.0 copy-done.5
  72.8 5.0 %finish.1 = (bf16[192,384]{1,0:T(8,128)(2,1)}, f32[192,384]{1,0:T(8,128)}, f32[192,2880]{1,0:T(8,128)}, f32[12,192]{1,0:T(8,128)}, f32[192,2880]{1,0:T(8,128)}, ...) custom-call(bf16[192,384]{1,0:T(8,128)(2,1)S(1)} %get-tuple-element., ...), custom_call_target="tpu_custom_call" | custom-call | tf_op jit(solution)/shard_map/finish/pallas_call | solution.py:1099
Async XLA Ops:
  0.6 72.1 %copy-start = (f32[192,2880]{1,0:T(8,128)S(1)}, f32[192,2880]{1,0:T(8,128)}, u32[]{:S(2)}) copy-start(f32[192,2880]{1,0:T(8,128)} %w_ref.1) | copy-start | bytes 6635524
  0.7 72.1 %copy-start.1 = (f32[192,2880]{1,0:T(8,128)S(1)}, f32[192,2880]{1,0:T(8,128)}, u32[]{:S(2)}) copy-start(f32[192,2880]{1,0:T(8,128)} %mom_ref.1) | copy-start | bytes 6635524
  0.7 72.1 %copy-start.2 = (f32[192,2880]{1,0:T(8,128)S(1)}, f32[192,2880]{1,0:T(8,128)}, u32[]{:S(2)}) copy-start(f32[192,2880]{1,0:T(8,128)} %squ_ref.1) | copy-start | bytes 6635524
  0.7 72.1 %copy-start.3 = (f32[12,192]{1,0:T(8,128)S(1)}, f32[12,192]{1,0:T(8,128)}, u32[]{:S(2)}) copy-start(f32[12,192]{1,0:T(8,128)} %v_ref.1) | copy-start | bytes 27652
  0.7 72.1 %copy-start.4 = (f32[12,192]{1,0:T(8,128)S(1)}, f32[12,192]{1,0:T(8,128)}, u32[]{:S(2)}) copy-start(f32[12,192]{1,0:T(8,128)} %mv_ref.1) | copy-start | bytes 27652
  0.7 72.1 %copy-start.5 = (f32[12,192]{1,0:T(8,128)S(1)}, f32[12,192]{1,0:T(8,128)}, u32[]{:S(2)}) copy-start(f32[12,192]{1,0:T(8,128)} %sv_ref.1) | copy-start | bytes 27652
